TPU v7x, 256 devices: a whole 4x4x8 slice. The times are simulated.
256 devices in a mesh: views: 16 (over z, x_hi), cols: 16 (over x_lo, y, core).
Axes of the slice: x: 4 (x_hi: 2, x_lo: 2; x = x_hi * 2 + x_lo), y: 4, z: 8, core: 2. Of those that a mesh axis runs over, the one named last changes fastest.
Arguments:
- light_field: bfloat16 [32, 32, 32, 2048], P('views', None, None, 'cols'), may hold values from -6 to 6
Outputs:
- depth_map: float32 [32, 32, 32, 2048], P('views', None, None, 'cols')
All inputs are finite; a program needn't handle non-finite values.
Results may differ from a plain program's by a relative error of at most 0.0003.
Values may be sent and summed in bfloat16 or wider, within the bound.
A program may use at most 128 MiB of HBM per device.

v0:
```python
import jax
import jax.numpy as jnp
from jax import lax
from jax.sharding import PartitionSpec as P


def extended_2(x, sides, width):
    for axis, dim in sides:
        devices, length = (lax.axis_size(axis), x.shape[dim])
        up = [(i, (i + 1) % devices) for i in range(devices - 1)]
        down = [(j, i) for i, j in up]
        last = lax.slice_in_dim(x, length - width, length, axis=dim)
        initial = lax.slice_in_dim(x, 0, width, axis=dim)
        before = lax.ppermute(last, axis, up)
        after = lax.ppermute(initial, axis, down)
        x = jnp.concatenate([before, x, after], axis=dim)
    return x


def shifted(field, axis, step):
    count = field.shape[axis]
    zshape = list(field.shape)
    zshape[axis] = abs(step)
    zeros = jnp.zeros(zshape, field.dtype)
    if step > 0:
        kept = lax.slice_in_dim(field, step, count, axis=axis)
        return jnp.concatenate([kept, zeros], axis=axis)
    kept = lax.slice_in_dim(field, 0, count + step, axis=axis)
    return jnp.concatenate([zeros, kept], axis=axis)


def derivative(field, axis):
    return (shifted(field, axis, 1) - shifted(field, axis, -1)) * 0.5


def smooth(field, axis):
    return 0.25 * shifted(field, axis, -1) + 0.5 * field + 0.25 * shifted(field, axis, 1)


def valid_smooth(field):
    return 0.25 * field[..., :-2] + 0.5 * field[..., 1:-1] + 0.25 * field[..., 2:]


def valid_smooth_lead(field):
    return 0.25 * field[:-2] + 0.5 * field[1:-1] + 0.25 * field[2:]


def slope_coherence(first, cross, second):
    slope = -cross / (second + 1.0)
    spread = (second - first) ** 2 + 4.0 * cross * cross
    coherence = spread / ((first + second) ** 2 + 1.0)
    return (slope, coherence)


def local(light_field):
    rows = light_field.shape[0]
    width = light_field.shape[3]
    start = lax.axis_index("cols") * width
    extended = extended_2(light_field, (("cols", 3),), 1).astype(jnp.float32)
    grad_v = derivative(extended[..., 1:-1], 1)
    grad_x = (extended[..., 2:] - extended[..., :-2]) * 0.5
    stacked = jnp.stack([smooth(c, 1) for c in (grad_v * grad_v, grad_v * grad_x, grad_x * grad_x)])
    bordered = extended_2(stacked, (("cols", 4),), 1)
    finished = valid_smooth(bordered)
    tensor_vv, tensor_vx, tensor_xx = (finished[0], finished[1], finished[2])
    slope_h, coh_h = slope_coherence(tensor_vv, tensor_vx, tensor_xx)
    deeper = extended_2(light_field, (("views", 0),), 2).astype(jnp.float32)
    grad_u = (deeper[2:] - deeper[:-2]) * 0.5
    grad_y = derivative(deeper[1:-1], 2)
    row_places = lax.axis_index("views") * rows - 1 + jnp.arange(rows + 2)
    row_keep = jnp.where(
        jnp.logical_and(row_places >= 0, row_places < rows * lax.axis_size("views")), 1.0, 0.0
    ).astype(jnp.float32)
    row_keep = row_keep.reshape((rows + 2, 1, 1, 1))
    comps = [
        valid_smooth_lead(smooth(c * row_keep, 2))
        for c in (grad_u * grad_u, grad_u * grad_y, grad_y * grad_y)
    ]
    slope_v, coh_v = slope_coherence(comps[0], comps[1], comps[2])
    joined = (coh_h * slope_h + coh_v * slope_v) / (coh_h + coh_v + 0.1)
    rimmed = extended_2(joined, (("cols", 3),), 1)
    left_part = rimmed[..., :-1]
    step_x = rimmed[..., 1:] - left_part
    step_y = shifted(left_part, 2, 1) - left_part
    scale = jnp.sqrt(step_x * step_x + step_y * step_y + 1.0)
    places = start - 1 + jnp.arange(width + 1)
    keep = jnp.where(places >= 0, 1.0, 0.0).astype(jnp.float32)
    flux_x = step_x / scale * keep
    flux_y = (step_y / scale)[..., 1:]
    spread = flux_x[..., 1:] - flux_x[..., :-1] + flux_y - shifted(flux_y, 2, -1)
    return joined + 0.2 * spread


def solution(mesh):
    return jax.shard_map(
        local,
        mesh=mesh,
        in_specs=(P("views", None, None, "cols"),),
        out_specs=P("views", None, None, "cols"),
        check_vma=False,
    )
```

profile of v0, /device:TPU:102, one launch (start us, length us, event | category | flops | bytes accessed | tf_op | source)
XLA Modules:
  0.0 98.1 jit_solution(760754455467094949)
XLA Ops:
  0.0 1.4 %fusion.37 = (bf16[2,32,32,1]{3,2,1,0:T(8,128)(2,1)S(1)}, bf16[2,32,32,1]{3,2,1,0:T(8,128)(2,1)S(1)}) fusion(bf16[2,32,32,128]{3,2,1,0:T(8,128)(2,1)} %param.1), kind=kLoop, calls=%fused_computation.83 | loop fusion | bytes 16384 | tf_op jit(solution)/shard_map/slice | solution.py:12
  1.4 4.6 %collective-permute-start.1 = (bf16[2,32,32,1]{3,2,1,0:T(8,128)(2,1)S(1)}, bf16[2,32,32,1]{3,2,1,0:T(8,128)(2,1)S(1)}, u32[]{:S(2)}, u32[]{:S(2)}) collective-permute-start(bf16[2,32,32,1]{3,2,1,0:T(8,128)(2,1)S(1)} %get-tuple-element.34), channel_id=1, source_target_pairs={{1,0},{2,1},{3,2},{4,3},{5,4},{6,5},{7,6},{8,7},{9,8},{10,9},{11,1... | collective-permute-start | bytes 12296 | tf_op jit(solution)/shard_map/ppermute | solution.py:15
  6.1 1.9 %collective-permute-start = (bf16[2,32,32,1]{3,2,1,0:T(8,128)(2,1)S(1)}, bf16[2,32,32,1]{3,2,1,0:T(8,128)(2,1)S(1)}, u32[]{:S(2)}, u32[]{:S(2)}) collective-permute-start(bf16[2,32,32,1]{3,2,1,0:T(8,128)(2,1)S(1)} %get-tuple-element.33), channel_id=1, source_target_pairs={{0,1},{1,2},{2,3},{3,4},{4,5},{5,6},{6,7},{7,8},{8,9},{9,10},{10,1... | collective-permute-start | bytes 12296 | tf_op jit(solution)/shard_map/ppermute | solution.py:14
  8.0 3.0 %collective-permute-start.5 = (bf16[2,32,32,128]{3,2,1,0:T(8,128)(2,1)}, bf16[2,32,32,128]{3,2,1,0:T(8,128)(2,1)}, u32[]{:S(2)}, u32[]{:S(2)}) collective-permute-start(bf16[2,32,32,128]{3,2,1,0:T(8,128)(2,1)} %param.1), channel_id=1, source_target_pairs={{16,0},{32,16},{48,32},{64,48},{80,64},{96,80},{112,96},{128,112},... | collective-permute-start | bytes 1572872 | tf_op jit(solution)/shard_map/ppermute | solution.py:15
  11.0 6.4 %collective-permute-start.4 = (bf16[2,32,32,128]{3,2,1,0:T(8,128)(2,1)}, bf16[2,32,32,128]{3,2,1,0:T(8,128)(2,1)}, u32[]{:S(2)}, u32[]{:S(2)}) collective-permute-start(bf16[2,32,32,128]{3,2,1,0:T(8,128)(2,1)} %param.1), channel_id=1, source_target_pairs={{0,16},{16,32},{32,48},{48,64},{64,80},{80,96},{96,112},{112,128},... | collective-permute-start | bytes 1572872 | tf_op jit(solution)/shard_map/ppermute | solution.py:14
  17.5 0.0 collective-permute-done.1
  17.5 17.9 %collective-permute-done = bf16[2,32,32,1]{3,2,1,0:T(8,128)(2,1)S(1)} collective-permute-done((bf16[2,32,32,1]{3,2,1,0:T(8,128)(2,1)S(1)}, bf16[2,32,32,1]{3,2,1,0:T(8,128)(2,1)S(1)}, u32[]{:S(2)}, u32[]{:S(2)}) %collective-permute-start) | collective-permute-done | bytes 4128 | tf_op jit(solution)/shard_map/ppermute | solution.py:14
  35.4 1.6 %maximum_convert_fusion.1 = f32[2,32,32,130]{3,2,1,0:T(8,128)S(1)} fusion(bf16[2,32,32,1]{3,2,1,0:T(8,128)(2,1)S(1)} %collective-permute-done.1, bf16[2,32,32,128]{3,2,1,0:T(8,128)(2,1)} %param.1, bf16[2,32,32,1]{3,2,1,0:T(8,128)(2,1)S(1)} %collective-permute-done), kind=kLoop, calls=%fused_computation.59 | loop fusion | flops 1597440 | bytes 1597440 | tf_op jit(solution)/shard_map/convert_element_type | solution.py:59
  37.0 0.6 fusion.29
  37.6 0.5 fusion.24
  38.1 0.3 fusion.36
  38.4 0.3 fusion.35
  38.7 0.2 fusion.34
  38.9 0.4 add_bitcast_fusion.2
  39.3 0.0 copy-start
  39.3 0.8 add_bitcast_fusion
  40.1 0.0 copy-start.1
  40.1 0.0 copy-start.2
  40.1 0.3 copy-done
  40.4 0.6 copy-done.1
  41.1 0.3 copy-done.2
  41.4 0.3 pad_maximum_fusion.6
  41.7 2.7 %fusion.27 = (f32[3,2,32,32,1]{4,3,2,1,0:T(8,128)S(1)}, f32[3,2,32,32,1]{4,3,2,1,0:T(8,128)}) fusion(f32[3,2,32,32,128]{4,3,2,1,0:T(8,128)S(1)} %pad_maximum_fusion.6), kind=kLoop, calls=%fused_computation.73 | loop fusion | bytes 98304 | tf_op jit(solution)/shard_map/slice | solution.py:12
  44.4 2.7 %copy.35 = f32[3,2,32,32,1]{3,2,4,1,0:T(8,128)S(1)} copy(f32[3,2,32,32,1]{4,3,2,1,0:T(8,128)} %get-tuple-element.11) | data formatting | bytes 49152 | tf_op jit(solution)/shard_map/slice | solution.py:13
  47.1 1.9 %collective-permute-start.3 = (f32[3,2,32,32,1]{3,2,4,1,0:T(8,128)S(1)}, f32[3,2,32,32,1]{3,2,4,1,0:T(8,128)S(1)}, u32[]{:S(2)}, u32[]{:S(2)}) collective-permute-start(f32[3,2,32,32,1]{3,2,4,1,0:T(8,128)S(1)} %copy.35), channel_id=1, source_target_pairs={{1,0},{2,1},{3,2},{4,3},{5,4},{6,5},{7,6},{8,7},{9,8},{10,9},{11,1... | collective-permute-start | bytes 73736 | tf_op jit(solution)/shard_map/ppermute | solution.py:15
  49.0 1.5 %copy.33 = f32[3,2,32,32,1]{3,2,4,1,0:T(8,128)S(1)} copy(f32[3,2,32,32,1]{4,3,2,1,0:T(8,128)S(1)} %get-tuple-element.10) | data formatting | bytes 49152 | tf_op jit(solution)/shard_map/slice | solution.py:12
  50.5 2.6 %collective-permute-start.2 = (f32[3,2,32,32,1]{3,2,4,1,0:T(8,128)S(1)}, f32[3,2,32,32,1]{3,2,4,1,0:T(8,128)S(1)}, u32[]{:S(2)}, u32[]{:S(2)}) collective-permute-start(f32[3,2,32,32,1]{3,2,4,1,0:T(8,128)S(1)} %copy.33), channel_id=1, source_target_pairs={{0,1},{1,2},{2,3},{3,4},{4,5},{5,6},{6,7},{7,8},{8,9},{9,10},{10,1... | collective-permute-start | bytes 73736 | tf_op jit(solution)/shard_map/ppermute | solution.py:14
  53.1 0.0 collective-permute-done.3
  53.1 1.3 %copy.36 = f32[3,2,32,32,1]{4,3,2,1,0:T(8,128)S(1)} copy(f32[3,2,32,32,1]{3,2,4,1,0:T(8,128)S(1)} %collective-permute-done.3) | data formatting | bytes 49152 | tf_op jit(solution)/shard_map/ppermute | solution.py:15
  54.4 4.1 %collective-permute-done.2 = f32[3,2,32,32,1]{3,2,4,1,0:T(8,128)S(1)} collective-permute-done((f32[3,2,32,32,1]{3,2,4,1,0:T(8,128)S(1)}, f32[3,2,32,32,1]{3,2,4,1,0:T(8,128)S(1)}, u32[]{:S(2)}, u32[]{:S(2)}) %collective-permute-start.2) | collective-permute-done | bytes 24608 | tf_op jit(solution)/shard_map/ppermute | solution.py:14
  58.5 2.4 %copy.34 = f32[3,2,32,32,1]{4,3,2,1,0:T(8,128)} copy(f32[3,2,32,32,1]{3,2,4,1,0:T(8,128)S(1)} %collective-permute-done.2) | data formatting | bytes 49152 | tf_op jit(solution)/shard_map/ppermute | solution.py:14
  61.0 7.9 %fusion.1 = f32[3,2,32,32,128]{4,3,2,1,0:T(8,128)S(1)} fusion(f32[3,2,32,32,1]{4,3,2,1,0:T(8,128)S(1)} %copy.36, f32[1,2,32,32,128]{4,3,2,1,0:T(8,128)} %copy-done.1, f32[1,2,32,32,128]{4,3,2,1,0:T(8,128)} %copy-done.2, f32[1,2,32,32,128]{4,3,2,1,0:T(8,128)} %copy-done, f32[3,2,32,32,1]{4,3,2,1,0:T(8,128)} %copy.34), kind=kLoop, calls=%fused_computation.2 | loop fusion | flops 10223616 | bytes 6340608 | tf_op jit(solution)/shard_map/add | solution.py:41
  68.9 0.0 collective-permute-done.5
  68.9 0.0 collective-permute-done.4
  68.9 1.6 %maximum_convert_fusion = f32[6,32,32,128]{3,2,1,0:T(8,128)S(1)} fusion(bf16[2,32,32,128]{3,2,1,0:T(8,128)(2,1)} %collective-permute-done.5, bf16[2,32,32,128]{3,2,1,0:T(8,128)(2,1)} %param.1, bf16[2,32,32,128]{3,2,1,0:T(8,128)(2,1)} %collective-permute-done.4), kind=kLoop, calls=%fused_computation.29 | loop fusion | flops 2359296 | bytes 4718592 | tf_op jit(solution)/shard_map/convert_element_type | solution.py:67
  70.5 0.4 fusion.28
  71.0 1.1 %multiply_multiply_fusion.2 = (f32[4,32,32,128]{3,2,1,0:T(8,128)S(1)}, f32[4,32,32,128]{3,2,1,0:T(8,128)S(1)}, f32[4,32,32,128]{3,2,1,0:T(8,128)S(1)}) fusion(f32[4]{0:T(128)S(1)} %and_select_fusion, f32[4,32,31,128]{3,2,1,0:T(8,128)S(1)} %get-tuple-element.13, f32[4,32,31,128]{3,2,1,0:T(8,128)S(1)} %get-tuple-element.12, ...), kind=kLoop, calls=%fused_computation.27 | loop fusion | flops 5242880 | bytes 14549008 | tf_op jit(solution)/shard_map/mul | solution.py:76
  72.1 0.7 fusion.32
  72.8 1.8 %fusion.30 = (f32[4,32,31,128]{3,2,1,0:T(8,128)S(1)}, f32[4,32,31,128]{3,2,1,0:T(8,128)}) fusion(f32[4,32,32,128]{3,2,1,0:T(8,128)S(1)} %get-tuple-element.9), kind=kLoop, calls=%fused_computation.76 | loop fusion | bytes 8126464 | tf_op jit(solution)/shard_map/slice | solution.py:28
  74.6 0.6 fusion.31
  75.2 0.8 multiply_add_fusion.2
  76.0 3.2 %multiply_add_fusion = (f32[4,32,32,128]{3,2,1,0:T(8,128)S(1)}, f32[4,32,32,128]{3,2,1,0:T(8,128)S(1)}) fusion(f32[4,32,31,128]{3,2,1,0:T(8,128)S(1)} %get-tuple-element.23, f32[4,32,32,128]{3,2,1,0:T(8,128)S(1)} %get-tuple-element.8, f32[4,32,31,128]{3,2,1,0:T(8,128)S(1)} %get-tuple-element.22, f32[4,32,31,128]{3,2,1,0:T(8,128)} %get-tuple-element.19, ...), kind=kLoop, calls=%fused_computation.22 | loop fusion | flops 5242880 | bytes 16515072 | tf_op jit(solution)/shard_map/add | solution.py:37
  79.2 1.8 %fusion.23 = f32[2,32,32,128]{3,2,1,0:T(8,128)S(1)} fusion(f32[4,32,32,128]{3,2,1,0:T(8,128)S(1)} %get-tuple-element.37, f32[4,32,32,128]{3,2,1,0:T(8,128)S(1)} %multiply_add_fusion.2, f32[4,32,32,128]{3,2,1,0:T(8,128)S(1)} %get-tuple-element.38, f32[3,2,32,32,128]{4,3,2,1,0:T(8,128)S(1)} %fusion.1), kind=kLoop, calls=%fused_computation.63 | loop fusion | flops 11796480 | bytes 13631488 | tf_op jit(solution)/shard_map/div | solution.py:80
  81.0 0.4 fusion.33
  81.4 0.4 copy.39
  81.8 1.9 %collective-permute-start.7 = (f32[2,32,32,1]{2,1,3,0:T(8,128)S(1)}, f32[2,32,32,1]{2,1,3,0:T(8,128)S(1)}, u32[]{:S(2)}, u32[]{:S(2)}) collective-permute-start(f32[2,32,32,1]{2,1,3,0:T(8,128)S(1)} %copy.39), channel_id=1, source_target_pairs={{0,1},{1,2},{2,3},{3,4},{4,5},{5,6},{6,7},{7,8},{8,9},{9,10},{10,1... | collective-permute-start | bytes 24584 | tf_op jit(solution)/shard_map/ppermute | solution.py:14
  83.8 0.4 copy.37
  84.2 6.0 %collective-permute-start.6 = (f32[2,32,32,1]{2,1,3,0:T(8,128)S(1)}, f32[2,32,32,1]{2,1,3,0:T(8,128)S(1)}, u32[]{:S(2)}, u32[]{:S(2)}) collective-permute-start(f32[2,32,32,1]{2,1,3,0:T(8,128)S(1)} %copy.37), channel_id=1, source_target_pairs={{1,0},{2,1},{3,2},{4,3},{5,4},{6,5},{7,6},{8,7},{9,8},{10,9},{11,1... | collective-permute-start | bytes 24584 | tf_op jit(solution)/shard_map/ppermute | solution.py:15
  90.2 0.0 collective-permute-done.7
  90.2 0.5 copy.40
  90.6 2.0 %fusion.4 = f32[2,32,31,129]{3,2,1,0:T(8,128)} fusion(f32[2,32,32,1]{3,2,1,0:T(8,128)S(1)} %copy.40, f32[2,32,32,128]{3,2,1,0:T(8,128)S(1)} %fusion.23), kind=kLoop, calls=%fused_computation.14 | loop fusion | flops 255936 | bytes 2080512 | tf_op jit(solution)/shard_map/concatenate | solution.py:16
  92.6 0.0 collective-permute-done.6
  92.6 0.5 copy.38
  93.1 3.1 %divide_multiply_fusion = (f32[2,32,32,129]{3,2,1,0:T(8,128)S(1)}, f32[2,32,32,129]{3,2,1,0:T(8,128)S(1)}) fusion(f32[129]{0:T(256)S(1)} %compare_select_fusion, f32[2,32,32,128]{3,2,1,0:T(8,128)S(1)} %fusion.23, f32[2,32,32,1]{3,2,1,0:T(8,128)S(1)} %copy.40, f32[2,32,32,1]{3,2,1,0:T(8,128)S(1)} %copy.38, f32[2,32,31,129]{3,2,1,0:T(8,128)} %fusion.4), kind=kLoop, calls=%fused_computation.18 | loop fusion | flops 2906112 | bytes 4202756 | tf_op jit(solution)/shard_map/mul | solution.py:88
  96.1 0.3 slice.234
  96.5 1.6 %fusion.13 = f32[2,32,32,128]{3,2,1,0:T(8,128)} fusion(f32[2,32,32,128]{3,2,1,0:T(8,128)S(1)} %fusion.23, f32[2,32,32,129]{3,2,1,0:T(8,128)S(1)} %get-tuple-element.6, f32[2,32,32,129]{3,2,1,0:T(8,128)S(1)} %get-tuple-element.5, f32[2,32,31,128]{3,2,1,0:T(8,128)S(1)} %slice.234), kind=kLoop, calls=%fused_computation.39 | loop fusion | flops 1310720 | bytes 6258688 | tf_op jit(solution)/shard_map/add | solution.py:91
  (2 shorter events, 0.0 us)
Async XLA Ops:
  1.4 16.1 %collective-permute-start.1 = (bf16[2,32,32,1]{3,2,1,0:T(8,128)(2,1)S(1)}, bf16[2,32,32,1]{3,2,1,0:T(8,128)(2,1)S(1)}, u32[]{:S(2)}, u32[]{:S(2)}) collective-permute-start(bf16[2,32,32,1]{3,2,1,0:T(8,128)(2,1)S(1)} %get-tuple-element.34), channel_id=1, source_target_pairs={{1,0},{2,1},{3,2},{4,3},{5,4},{6,5},{7,6},{8,7},{9,8},{10,9},{11,1... | collective-permute-start | bytes 12296 | tf_op jit(solution)/shard_map/ppermute | solution.py:15
  6.1 29.3 %collective-permute-start = (bf16[2,32,32,1]{3,2,1,0:T(8,128)(2,1)S(1)}, bf16[2,32,32,1]{3,2,1,0:T(8,128)(2,1)S(1)}, u32[]{:S(2)}, u32[]{:S(2)}) collective-permute-start(bf16[2,32,32,1]{3,2,1,0:T(8,128)(2,1)S(1)} %get-tuple-element.33), channel_id=1, source_target_pairs={{0,1},{1,2},{2,3},{3,4},{4,5},{5,6},{6,7},{7,8},{8,9},{9,10},{10,1... | collective-permute-start | bytes 12296 | tf_op jit(solution)/shard_map/ppermute | solution.py:14
  8.0 60.9 %collective-permute-start.5 = (bf16[2,32,32,128]{3,2,1,0:T(8,128)(2,1)}, bf16[2,32,32,128]{3,2,1,0:T(8,128)(2,1)}, u32[]{:S(2)}, u32[]{:S(2)}) collective-permute-start(bf16[2,32,32,128]{3,2,1,0:T(8,128)(2,1)} %param.1), channel_id=1, source_target_pairs={{16,0},{32,16},{48,32},{64,48},{80,64},{96,80},{112,96},{128,112},... | collective-permute-start | bytes 1572872 | tf_op jit(solution)/shard_map/ppermute | solution.py:15
  11.0 57.9 %collective-permute-start.4 = (bf16[2,32,32,128]{3,2,1,0:T(8,128)(2,1)}, bf16[2,32,32,128]{3,2,1,0:T(8,128)(2,1)}, u32[]{:S(2)}, u32[]{:S(2)}) collective-permute-start(bf16[2,32,32,128]{3,2,1,0:T(8,128)(2,1)} %param.1), channel_id=1, source_target_pairs={{0,16},{16,32},{32,48},{48,64},{64,80},{80,96},{96,112},{112,128},... | collective-permute-start | bytes 1572872 | tf_op jit(solution)/shard_map/ppermute | solution.py:14
  39.3 1.1 %copy-start = (f32[1,2,32,32,128]{4,3,2,1,0:T(8,128)}, f32[1,2,32,32,128]{4,3,2,1,0:T(8,128)S(1)}, u32[]{:S(2)}) copy-start(f32[1,2,32,32,128]{4,3,2,1,0:T(8,128)S(1)} %add_bitcast_fusion.2) | copy-start | bytes 3145732
  40.1 1.0 copy-start.1
  40.1 1.3 %copy-start.2 = (f32[1,2,32,32,128]{4,3,2,1,0:T(8,128)}, f32[1,2,32,32,128]{4,3,2,1,0:T(8,128)S(1)}, u32[]{:S(2)}) copy-start(f32[1,2,32,32,128]{4,3,2,1,0:T(8,128)S(1)} %get-tuple-element.36) | copy-start | bytes 3145732
  47.1 6.0 %collective-permute-start.3 = (f32[3,2,32,32,1]{3,2,4,1,0:T(8,128)S(1)}, f32[3,2,32,32,1]{3,2,4,1,0:T(8,128)S(1)}, u32[]{:S(2)}, u32[]{:S(2)}) collective-permute-start(f32[3,2,32,32,1]{3,2,4,1,0:T(8,128)S(1)} %copy.35), channel_id=1, source_target_pairs={{1,0},{2,1},{3,2},{4,3},{5,4},{6,5},{7,6},{8,7},{9,8},{10,9},{11,1... | collective-permute-start | bytes 73736 | tf_op jit(solution)/shard_map/ppermute | solution.py:15
  50.5 8.0 %collective-permute-start.2 = (f32[3,2,32,32,1]{3,2,4,1,0:T(8,128)S(1)}, f32[3,2,32,32,1]{3,2,4,1,0:T(8,128)S(1)}, u32[]{:S(2)}, u32[]{:S(2)}) collective-permute-start(f32[3,2,32,32,1]{3,2,4,1,0:T(8,128)S(1)} %copy.33), channel_id=1, source_target_pairs={{0,1},{1,2},{2,3},{3,4},{4,5},{5,6},{6,7},{7,8},{8,9},{9,10},{10,1... | collective-permute-start | bytes 73736 | tf_op jit(solution)/shard_map/ppermute | solution.py:14
  81.8 8.4 %collective-permute-start.7 = (f32[2,32,32,1]{2,1,3,0:T(8,128)S(1)}, f32[2,32,32,1]{2,1,3,0:T(8,128)S(1)}, u32[]{:S(2)}, u32[]{:S(2)}) collective-permute-start(f32[2,32,32,1]{2,1,3,0:T(8,128)S(1)} %copy.39), channel_id=1, source_target_pairs={{0,1},{1,2},{2,3},{3,4},{4,5},{5,6},{6,7},{7,8},{8,9},{9,10},{10,1... | collective-permute-start | bytes 24584 | tf_op jit(solution)/shard_map/ppermute | solution.py:14
  84.2 8.4 %collective-permute-start.6 = (f32[2,32,32,1]{2,1,3,0:T(8,128)S(1)}, f32[2,32,32,1]{2,1,3,0:T(8,128)S(1)}, u32[]{:S(2)}, u32[]{:S(2)}) collective-permute-start(f32[2,32,32,1]{2,1,3,0:T(8,128)S(1)} %copy.37), channel_id=1, source_target_pairs={{1,0},{2,1},{3,2},{4,3},{5,4},{6,5},{7,6},{8,7},{9,8},{10,9},{11,1... | collective-permute-start | bytes 24584 | tf_op jit(solution)/shard_map/ppermute | solution.py:15
where the time goes:
time: 98.6 us; the launch traced here: 98.1 us
  starting transfers between devices  28.4 us (29%)
  other arithmetic  26.7 us (27%)
  waiting for transfers between devices  22 us (22%)
  local copies, waits for them, and re-layouts  20.7 us (21%)
    ppermute x4, waiting for transfers between devices, extended_2(): before = lax.ppermute(last, axis, up)  22 us
    ppermute x4, starting transfers between devices, extended_2(): after = lax.ppermute(initial, axis, down)  15.5 us
    ppermute x4, starting transfers between devices, extended_2(): before = lax.ppermute(last, axis, up)  12.9 us
    add x1, other arithmetic, valid_smooth(): 0.25 * field[..., :-2] + 0.5 * field[..., 1:-1] + 0.25 * field[..., 2:]  7.92 us
    slice x4, local copies, waits for them, and re-layouts, extended_2(): last = lax.slice_in_dim(x, length - width, length, axis=dim)  6.03 us
    slice x7, local copies, waits for them, and re-layouts, shifted(): kept = lax.slice_in_dim(field, 0, count + step, axis=axis)  4.23 us
    add x2, other arithmetic, smooth(): 0.25 * shifted(field, axis, -1) + 0.5 * field  3.98 us
    slice x3, local copies, waits for them, and re-layouts, extended_2(): initial = lax.slice_in_dim(x, 0, width, axis=dim)  3.46 us
  transfers between devices with their start and end apart: 8, of which 2 were waited for; matrix products, arithmetic and copies ran while one was open for 27% of the time, Pallas kernels for 0%

commit v1 on v0

v1 whole, which is shorter than its diff:
```python
import functools

import jax
import jax.numpy as jnp
from jax import lax
from jax.experimental import pallas as pl
from jax.experimental.pallas import tpu as pltpu
from jax.sharding import PartitionSpec as P

MESH = pl.DeviceIdType.MESH
F32 = jnp.float32
BF16 = jnp.bfloat16
ROWS, V, Y, X = 2, 32, 32, 128
CHUNK = 4
CHUNKS = V // CHUNK
STEP = 2
PLANE = V * Y


def recip(x):
    r = pl.reciprocal(x, approx=True)
    return r * (2.0 - x * r)


def measures(first, cross, second):
    apart = second - first
    whole = second + first
    twice = cross + cross
    return apart * apart + twice * twice, whole * whole + 4096.0, cross, second + 64.0


def weighted(first, cross, second):
    spread, energy, cross, pivot = measures(first, cross, second)
    part = spread * recip(energy * pivot)
    return part * pivot + 0.1, part * cross


def join(weight_h, moment_h, first, cross, second):
    spread, energy, cross, pivot = measures(first, cross, second)
    above = moment_h * (energy * pivot) + spread * cross
    below = pivot * (energy * weight_h + spread)
    return -(above * recip(below))


def kernel(
    nv,
    nc,
    f_hbm,
    o_hbm,
    fv,
    full,
    got,
    wide,
    weight,
    moment,
    fix,
    out,
    pack,
    pack_l,
    pack_r,
    mid,
    mids,
    edge,
    edge_j,
    edge_d,
    load_sem,
    near_s,
    near_r,
    far_s,
    far_r,
    pack_s,
    pack_rs,
    mid_s,
    mid_r,
    out_s,
):
    vi = lax.axis_index("views")
    cj = lax.axis_index("cols")
    odd = lax.rem(vi, 2)
    even = 1 - odd
    partner = vi + 1 - 2 * odd
    ahead = lax.rem(vi + nv + 2 - 4 * odd, nv)
    behind = lax.rem(vi + nv - 2 + 4 * odd, nv)
    left = lax.rem(cj + nc - 1, nc)
    right = lax.rem(cj + 1, nc)
    at_top = vi == 0
    at_bottom = vi == nv - 1
    has_far = jnp.logical_and(vi > 0, vi < nv - 1)
    sends_far = jnp.logical_and(vi != nv - 2, vi != 1)

    barrier = pltpu.get_barrier_semaphore()
    for there in ((partner, cj), (behind, cj), (vi, left), (vi, right)):
        pl.semaphore_signal(barrier, inc=1, device_id=there, device_id_type=MESH)

    load = pltpu.make_async_copy(f_hbm, fv, load_sem)
    load.start()
    load.wait()

    row8 = lax.broadcasted_iota(jnp.int32, (8, PLANE), 0)
    row16 = lax.broadcasted_iota(jnp.int32, (16, X), 0)
    lane16 = lax.broadcasted_iota(jnp.int32, (16, X), 1)
    r8 = lax.rem(row16, 8)
    wanted = jnp.where(r8 < 4, r8 + (X - 4), r8 - 4)

    packed = jnp.zeros((16, PLANE), F32)
    for u in range(ROWS):
        pick = jnp.where(jnp.logical_and(lane16 == wanted, row16 // 8 == u), 1.0, 0.0).astype(BF16)
        packed = packed + lax.dot_general(
            pick, fv[u].reshape(PLANE, X), (((1,), (1,)), ((), ())), preferred_element_type=F32
        )
    pack[...] = packed.astype(BF16)

    pl.semaphore_wait(barrier, 4)

    def remote(src, dst, s, r, there):
        return pltpu.make_async_remote_copy(
            src_ref=src, dst_ref=dst, send_sem=s, recv_sem=r, device_id=there, device_id_type=MESH
        )

    def near(k):
        span = pl.ds(k * CHUNK, CHUNK)
        return remote(fv.at[:, span], got.at[odd, :, span], near_s.at[k], near_r.at[k], (partner, cj))

    def near_in(k):
        span = pl.ds(k * CHUNK, CHUNK)
        return remote(fv.at[:, span], got.at[even, :, span], near_s.at[k], near_r.at[k], (partner, cj))

    def far(k):
        span = pl.ds(k * CHUNK, CHUNK)
        return remote(got.at[even, :, span], got.at[odd, :, span], far_s.at[k], far_r.at[k], (ahead, cj))

    to_left = remote(pack, pack_r, pack_s.at[0], pack_rs.at[0], (vi, left))
    to_right = remote(pack, pack_l, pack_s.at[1], pack_rs.at[1], (vi, right))
    to_left.start()
    to_right.start()
    for k in range(CHUNKS):
        near(k).start()

    @pl.when(at_top)
    def _():
        got[0, 0] = fv[0]
        got[0, 1] = jnp.zeros((V, Y, X), BF16)

    @pl.when(at_bottom)
    def _():
        got[1, 0] = jnp.zeros((V, Y, X), BF16)
        got[1, 1] = fv[1]

    def lanes(a, k):
        return pltpu.roll(a, (-k) % a.shape[-1], a.ndim - 1)

    def smooth_lanes(a):
        pair = a + lanes(a, -1)
        return pair + lanes(pair, 1)

    def horizontal(i, carry):
        u = i // 2
        rows = pl.ds(pl.multiple_of(lax.rem(i, 2) * 16, 16), 16)
        nothing = jnp.zeros((16, X), F32)
        field = [fv[u, v, rows, :].astype(F32) for v in range(V)]
        for v in range(V):
            full[u, v, rows, :] = field[v]
        pairs, last = None, (nothing,) * 3
        for v in range(V + 1):
            if v < V:
                grad_v = (field[v + 1] if v + 1 < V else nothing) - (field[v - 1] if v else nothing)
                grad_x = lanes(field[v], 1) - lanes(field[v], -1)
                now = tuple(smooth_lanes(c) for c in (grad_v * grad_v, grad_v * grad_x, grad_x * grad_x))
            else:
                now = (nothing,) * 3
            sums = tuple(a + b for a, b in zip(last, now))
            if v:
                w, m = weighted(*(a + b for a, b in zip(pairs, sums)))
                weight[u, v - 1, rows, :] = w
                moment[u, v - 1, rows, :] = m
            pairs, last = sums, now
        return carry

    lax.fori_loop(0, 2, horizontal, 0)

    to_left.wait_recv()
    to_right.wait_recv()
    first, final = cj == 0, cj == nc - 1
    own = pack[...].astype(F32)
    from_l = pack_l[...].astype(F32)
    from_r = pack_r[...].astype(F32)
    mixed = []
    for u in range(ROWS):
        mine = own[8 * u : 8 * u + 8]
        l_in = from_l[8 * u : 8 * u + 8]
        r_in = from_r[8 * u : 8 * u + 8]
        flip_l = jnp.where(row8 == 2, pltpu.roll(mine, 6, 0), 0.0)
        flip_r = jnp.where(row8 == 5, pltpu.roll(mine, 2, 0), 0.0)
        l_in = jnp.where(first, flip_l, l_in)
        r_in = jnp.where(final, flip_r, r_in)
        e_l = jnp.where(row8 < 4, l_in, mine)
        e_r = jnp.where(row8 < 4, mine, r_in)
        edge[0, 2 + u] = e_l
        edge[1, 2 + u] = e_r
        mixed.append(jnp.where(jnp.logical_and(row8 >= 2, row8 < 6), e_l, pltpu.roll(e_r, 4, 0)))
    mid[...] = jnp.concatenate(mixed, axis=0).astype(BF16)
    mid_near = remote(mid, mids.at[odd], mid_s.at[0], mid_r.at[0], (partner, cj))
    mid_near_in = remote(mid, mids.at[even], mid_s.at[0], mid_r.at[0], (partner, cj))
    mid_far = remote(mids.at[even], mids.at[odd], mid_s.at[1], mid_r.at[1], (ahead, cj))
    mid_near.start()

    lax.fori_loop(2, 4, horizontal, 0)

    mid_near_in.wait_recv()

    @pl.when(sends_far)
    def _():
        mid_far.start()

    near_in(0).wait_recv()

    @pl.when(sends_far)
    def _():
        far(0).start()

    @pl.when(has_far)
    def _():
        mid_far.wait_recv()

    for slot in range(2):
        rows_in = mids[slot].astype(F32)
        for u in range(ROWS):
            tile = rows_in[8 * u : 8 * u + 8]
            edge[0, 4 * slot + u] = tile
            edge[1, 4 * slot + u] = pltpu.roll(tile, 4, 0)

    @pl.when(at_top)
    def _():
        for side in range(2):
            edge[side, 0] = edge[side, 2]
            edge[side, 1] = jnp.zeros((8, PLANE), F32)

    @pl.when(at_bottom)
    def _():
        for side in range(2):
            edge[side, 4] = jnp.zeros((8, PLANE), F32)
            edge[side, 5] = edge[side, 3]

    place = lax.broadcasted_iota(jnp.int32, (8, PLANE), 1)
    y_at = lax.rem(place, Y)

    def cols_by(a, k):
        return pltpu.roll(a, (-k) % 8, 0)

    def y_by(a, k):
        return jnp.where(y_at == (Y - 1 if k > 0 else 0), 0.0, pltpu.roll(a, (-k) % PLANE, 1))

    def v_by(a, k):
        return jnp.where(
            place >= PLANE - Y if k > 0 else place < Y, 0.0, pltpu.roll(a, (-k * Y) % PLANE, 1)
        )

    def smooth_by(by, a):
        return by(a, -1) + (a + a) + by(a, 1)

    def edges(side, carry):
        j_below = jnp.where(jnp.logical_and(final, side == 1), 4, 8)
        q_from = jnp.where(jnp.logical_and(first, side == 0), 4, 0)
        tiles = [edge[side, r] for r in range(6)]
        comps = []
        for r in range(1, 5):
            grad_u = tiles[r + 1] - tiles[r - 1]
            grad_y = y_by(tiles[r], 1) - y_by(tiles[r], -1)
            comps.append((grad_u * grad_u, grad_u * grad_y, grad_y * grad_y))
        for u in range(ROWS):
            f = tiles[2 + u]
            grad_v = v_by(f, 1) - v_by(f, -1)
            grad_x = cols_by(f, 1) - cols_by(f, -1)
            w, m = weighted(
                *(
                    smooth_by(v_by, smooth_by(cols_by, c))
                    for c in (grad_v * grad_v, grad_v * grad_x, grad_x * grad_x)
                )
            )
            tensor = [
                smooth_by(y_by, a + (b + b) + c) for a, b, c in zip(comps[u], comps[u + 1], comps[u + 2])
            ]
            joined = jnp.where(row8 < j_below, join(w, m, *tensor), 0.0)
            step_x = cols_by(joined, 1) - joined
            step_y = y_by(joined, 1) - joined
            scale = lax.rsqrt(step_x * step_x + step_y * step_y + 1.0)
            flux_x = jnp.where(row8 >= q_from, step_x * scale, 0.0)
            flux_y = step_y * scale
            depth = joined + 0.2 * (flux_x - cols_by(flux_x, -1) + flux_y - y_by(flux_y, -1))
            edge_j[side, u] = pltpu.roll(joined, 4, 0)
            edge_d[side, u] = pltpu.roll(depth, 5, 0)
        return carry

    lax.fori_loop(0, 2, edges, 0)

    small = lax.broadcasted_iota(jnp.int32, (8, X), 0)

    def spread_out(u, carry):
        for b in range(PLANE // X):
            part = pl.ds(b * X, X)
            both = jnp.where(small == 0, edge_d[1, u, :, part], edge_d[0, u, :, part])
            block = jnp.concatenate(
                [
                    edge_j[0, u, :, part],
                    jnp.zeros((56, X), F32),
                    both,
                    jnp.zeros((48, X), F32),
                    edge_j[1, u, :, part],
                ],
                axis=0,
            )
            fix[u, pl.ds(4 * b, 4)] = block.T.reshape(4, Y, X)
        return carry

    lax.fori_loop(0, 2, spread_out, 0)

    lane = lax.broadcasted_iota(jnp.int32, (STEP, 8, X), 2)
    sub = lax.broadcasted_iota(jnp.int32, (STEP, 8, X), 1)
    rim = jnp.logical_or(lane < 2, lane >= X - 2)
    outer = jnp.logical_or(lane == 0, lane == X - 1)

    def parts(ref, *at):
        return [ref[(*at, pl.ds(p, 8, stride=4), slice(None))] for p in range(4)]

    def y_up(a, rest=0.0):
        return a[1:] + [jnp.where(sub == 7, rest, pltpu.roll(a[0], 7, 1))]

    def y_down(a):
        return [jnp.where(sub == 0, 0.0, pltpu.roll(a[3], 1, 1))] + a[:3]

    def smooth_y(a):
        pair = [b + c for b, c in zip(a, y_down(a))]
        return [b + c for b, c in zip(pair, y_up(pair, a[3]))]

    def vertical(v0):
        span = pl.ds(v0, STEP)
        for slot in range(2):
            for u in range(ROWS):
                wide[2 * slot + u] = got[slot, u, span].astype(F32)
        every = slice(None)
        field = (
            [parts(wide, 0, every), parts(wide, 1, every)]
            + [parts(full, u, span) for u in range(ROWS)]
            + [parts(wide, 2, every), parts(wide, 3, every)]
        )
        comps = []
        for r in range(1, 5):
            grad_u = [a - b for a, b in zip(field[r + 1], field[r - 1])]
            grad_y = [a - b for a, b in zip(y_up(field[r]), y_down(field[r]))]
            comps.append(
                [
                    [a * b for a, b in zip(g, h)]
                    for g, h in ((grad_u, grad_u), (grad_u, grad_y), (grad_y, grad_y))
                ]
            )
        pairs = [
            [[a + b for a, b in zip(c, d)] for c, d in zip(comps[r], comps[r + 1])] for r in range(3)
        ]
        for u in range(ROWS):
            tensor = [
                smooth_y([a + b for a, b in zip(c, d)]) for c, d in zip(pairs[u], pairs[u + 1])
            ]
            w, m, t = parts(weight, u, span), parts(moment, u, span), parts(fix, u, span)
            joined = [
                jnp.where(rim, t[p], join(w[p], m[p], *(c[p] for c in tensor))) for p in range(4)
            ]
            flux_x, flux_y = [], []
            for here, below in zip(joined, y_up(joined)):
                step_x = lanes(here, 1) - here
                step_y = below - here
                scale = lax.rsqrt(step_x * step_x + step_y * step_y + 1.0)
                flux_x.append(step_x * scale)
                flux_y.append(step_y * scale)
            for p, above in enumerate(y_down(flux_y)):
                depth = joined[p] + 0.2 * (flux_x[p] - lanes(flux_x[p], -1) + flux_y[p] - above)
                out[u, span, pl.ds(p, 8, stride=4), :] = jnp.where(outer, lanes(t[p], -63), depth)

    def stored(k):
        span = pl.ds(k * CHUNK, CHUNK)
        return pltpu.make_async_copy(out.at[:, span], o_hbm.at[:, span], out_s.at[k])

    def chunk(k, carry):
        @pl.when(k + 1 < CHUNKS)
        def _():
            near_in(k + 1).wait_recv()

            @pl.when(sends_far)
            def _():
                far(k + 1).start()

        @pl.when(has_far)
        def _():
            far(k).wait_recv()

        def inner(i, c):
            vertical(k * CHUNK + i * STEP)
            return c

        lax.fori_loop(0, CHUNK // STEP, inner, 0)
        stored(k).start()
        return carry

    lax.fori_loop(0, CHUNKS, chunk, 0)

    to_left.wait_send()
    to_right.wait_send()
    mid_near.wait_send()
    for k in range(CHUNKS):
        near(k).wait_send()

    @pl.when(sends_far)
    def _():
        mid_far.wait_send()
        for k in range(CHUNKS):
            far(k).wait_send()

    for k in range(CHUNKS):
        stored(k).wait()


def local(nv, nc, light_field):
    block = (ROWS, V, Y, X)
    dma = pltpu.SemaphoreType.DMA
    return pl.pallas_call(
        functools.partial(kernel, nv, nc),
        out_shape=jax.ShapeDtypeStruct(block, F32),
        in_specs=[pl.BlockSpec(memory_space=pl.ANY)],
        out_specs=pl.BlockSpec(memory_space=pl.ANY),
        scratch_shapes=[
            pltpu.VMEM(block, BF16),
            pltpu.VMEM(block, F32),
            pltpu.VMEM((2, *block), BF16),
            pltpu.VMEM((4, STEP, Y, X), F32),
            pltpu.VMEM(block, F32),
            pltpu.VMEM(block, F32),
            pltpu.VMEM(block, F32),
            pltpu.VMEM(block, F32),
            pltpu.VMEM((16, PLANE), BF16),
            pltpu.VMEM((16, PLANE), BF16),
            pltpu.VMEM((16, PLANE), BF16),
            pltpu.VMEM((16, PLANE), BF16),
            pltpu.VMEM((2, 16, PLANE), BF16),
            pltpu.VMEM((2, 6, 8, PLANE), F32),
            pltpu.VMEM((2, ROWS, 8, PLANE), F32),
            pltpu.VMEM((2, ROWS, 8, PLANE), F32),
            dma,
            dma((CHUNKS,)),
            dma((CHUNKS,)),
            dma((CHUNKS,)),
            dma((CHUNKS,)),
            dma((2,)),
            dma((2,)),
            dma((2,)),
            dma((2,)),
            dma((CHUNKS,)),
        ],
        compiler_params=pltpu.CompilerParams(
            collective_id=0, has_side_effects=True, vmem_limit_bytes=32 << 20
        ),
        cost_estimate=pl.CostEstimate(flops=60_000_000, bytes_accessed=1_600_000, transcendentals=800_000),
    )(light_field)


def solution(mesh):
    return jax.shard_map(
        functools.partial(local, mesh.shape["views"], mesh.shape["cols"]),
        mesh=mesh,
        in_specs=(P("views", None, None, "cols"),),
        out_specs=P("views", None, None, "cols"),
        check_vma=False,
    )
```

time: 98.6 us -> 47.2 us (0.48)
  the two profiles are of different devices: /device:TPU:102 before, /device:TPU:4 now
where the time goes in v1:
time: 47.2 us; the launch traced here: 47.1 us
  Pallas kernels  45 us (95%)
  local copies, waits for them, and re-layouts  2.01 us (4%)
    pallas_call x1, Pallas kernels, local(): pl.pallas_call(functools.partial(kernel, nv, nc), out_shape=jax.ShapeDtyp...  45 us
    unnamed x3, local copies, waits for them, and re-layouts  2.01 us

profile of v1, /device:TPU:4, one launch (start us, length us, event | category | flops | bytes accessed | tf_op | source)
XLA Modules:
  0.0 47.1 jit_solution(16518953201307277216)
XLA Ops:
  0.0 0.0 copy-start
  0.0 1.0 %copy-done = bf16[2,32,32,128]{3,2,1,0:T(8,128)(2,1)S(1)} copy-done((bf16[2,32,32,128]{3,2,1,0:T(8,128)(2,1)S(1)}, bf16[2,32,32,128]{3,2,1,0:T(8,128)(2,1)}, u32[]{:S(2)}) %copy-start) | copy-done | bytes 524312
  1.0 45.0 %shard_map.17 = f32[2,32,32,128]{3,2,1,0:T(8,128)S(1)} custom-call(bf16[2,32,32,128]{3,2,1,0:T(8,128)(2,1)S(1)} %copy-done), custom_call_target="tpu_custom_call" | custom-call | flops 60000000 | bytes 1600000 | tf_op jit(solution)/shard_map/pallas_call | solution.py:424
  46.1 1.0 %copy.3 = f32[2,32,32,128]{3,2,1,0:T(8,128)} copy(f32[2,32,32,128]{3,2,1,0:T(8,128)S(1)} %shard_map.17) | data formatting | bytes 2097152
Async XLA Ops:
  0.0 1.0 %copy-start = (bf16[2,32,32,128]{3,2,1,0:T(8,128)(2,1)S(1)}, bf16[2,32,32,128]{3,2,1,0:T(8,128)(2,1)}, u32[]{:S(2)}) copy-start(bf16[2,32,32,128]{3,2,1,0:T(8,128)(2,1)} %f_hbm.1) | copy-start | bytes 1572868

commit v2 on v1

--- a/solution.py
+++ b/solution.py
@@ -13,7 +13,11 @@
 ROWS, V, Y, X = 2, 32, 32, 128
 CHUNK = 4
 CHUNKS = V // CHUNK
-STEP = 2
+STEP = 4
+H_CHUNK = 8
+H_STEPS = V // H_CHUNK
+AHEAD = 3
+FIRST = 3
 PLANE = V * Y
 
 
@@ -46,7 +50,7 @@
     nv,
     nc,
     f_hbm,
-    o_hbm,
+    out,
     fv,
     full,
     got,
@@ -54,7 +58,6 @@
     weight,
     moment,
     fix,
-    out,
     pack,
     pack_l,
     pack_r,
@@ -72,7 +75,6 @@
     pack_rs,
     mid_s,
     mid_r,
-    out_s,
 ):
     vi = lax.axis_index("views")
     cj = lax.axis_index("cols")
@@ -133,7 +135,7 @@
     to_right = remote(pack, pack_l, pack_s.at[1], pack_rs.at[1], (vi, right))
     to_left.start()
     to_right.start()
-    for k in range(CHUNKS):
+    for k in range(FIRST):
         near(k).start()
 
     @pl.when(at_top)
@@ -154,29 +156,44 @@
         return pair + lanes(pair, 1)
 
     def horizontal(i, carry):
-        u = i // 2
-        rows = pl.ds(pl.multiple_of(lax.rem(i, 2) * 16, 16), 16)
-        nothing = jnp.zeros((16, X), F32)
-        field = [fv[u, v, rows, :].astype(F32) for v in range(V)]
-        for v in range(V):
-            full[u, v, rows, :] = field[v]
-        pairs, last = None, (nothing,) * 3
-        for v in range(V + 1):
-            if v < V:
-                grad_v = (field[v + 1] if v + 1 < V else nothing) - (field[v - 1] if v else nothing)
-                grad_x = lanes(field[v], 1) - lanes(field[v], -1)
-                now = tuple(smooth_lanes(c) for c in (grad_v * grad_v, grad_v * grad_x, grad_x * grad_x))
-            else:
-                now = (nothing,) * 3
-            sums = tuple(a + b for a, b in zip(last, now))
-            if v:
-                w, m = weighted(*(a + b for a, b in zip(pairs, sums)))
-                weight[u, v - 1, rows, :] = w
-                moment[u, v - 1, rows, :] = m
-            pairs, last = sums, now
-        return carry
-
-    lax.fori_loop(0, 2, horizontal, 0)
+        before, last = carry
+        u = i // H_STEPS
+        v0 = lax.rem(i, H_STEPS) * H_CHUNK
+        top = v0 == 0
+        before = [jnp.where(top, 0.0, c) for c in before]
+        last = [jnp.where(top, 0.0, c) for c in last]
+        here = fv[u, pl.ds(v0, H_CHUNK)].astype(F32)
+        full[u, pl.ds(v0, H_CHUNK)] = here
+        above = jnp.where(top, 0.0, fv[u, jnp.maximum(v0 - 1, 0)].astype(F32))
+        below = jnp.where(
+            v0 + H_CHUNK < V, fv[u, jnp.minimum(v0 + H_CHUNK, V - 1)].astype(F32), 0.0
+        )
+        mid_x = jnp.concatenate([above[None], here, below[None]], 0)
+        left_x, right_x = lanes(mid_x, -1), lanes(mid_x, 1)
+        grad_v = [a[2:] - a[:-2] for a in (left_x, mid_x, right_x)]
+        grad_x = [here - lanes(here, -2), right_x[1:-1] - left_x[1:-1], lanes(here, 2) - here]
+
+        def smooth_x(p, q):
+            a, b, c = (s * t for s, t in zip(p, q))
+            return (a + c) + (b + b)
+
+        now = [smooth_x(grad_v, grad_v), smooth_x(grad_v, grad_x), smooth_x(grad_x, grad_x)]
+        run = [jnp.concatenate([a[None], b[None], c], 0) for a, b, c in zip(before, last, now)]
+        pairs = [c[1:] + c[:-1] for c in run]
+        w, m = weighted(*(c[1:] + c[:-1] for c in pairs))
+        weight[u, pl.ds(v0, H_CHUNK)] = w
+        moment[u, pl.ds(v0, H_CHUNK)] = m
+
+        @pl.when(v0 == V - H_CHUNK)
+        def _():
+            w, m = weighted(*(c[-1] + d[-1] for c, d in zip(pairs, now)))
+            weight[u, V] = w
+            moment[u, V] = m
+
+        return [c[H_CHUNK - 2] for c in now], [c[H_CHUNK - 1] for c in now]
+
+    zeros = [jnp.zeros((Y, X), F32)] * 3
+    lax.fori_loop(0, H_STEPS, horizontal, (zeros, zeros))
 
     to_left.wait_recv()
     to_right.wait_recv()
@@ -203,20 +220,27 @@
     mid_near_in = remote(mid, mids.at[even], mid_s.at[0], mid_r.at[0], (partner, cj))
     mid_far = remote(mids.at[even], mids.at[odd], mid_s.at[1], mid_r.at[1], (ahead, cj))
     mid_near.start()
-
-    lax.fori_loop(2, 4, horizontal, 0)
-
+    for k in range(FIRST, CHUNKS):
+        near(k).start()
+
+    def relay(k):
+        near_in(k).wait_recv()
+
+        @pl.when(sends_far)
+        def _():
+            far(k).start()
+
+    lax.fori_loop(H_STEPS, 2 * H_STEPS, horizontal, (zeros, zeros))
+
+    relay(0)
+    relay(1)
     mid_near_in.wait_recv()
 
     @pl.when(sends_far)
     def _():
         mid_far.start()
 
-    near_in(0).wait_recv()
-
-    @pl.when(sends_far)
-    def _():
-        far(0).start()
+    relay(2)
 
     @pl.when(has_far)
     def _():
@@ -289,6 +313,7 @@
             depth = joined + 0.2 * (flux_x - cols_by(flux_x, -1) + flux_y - y_by(flux_y, -1))
             edge_j[side, u] = pltpu.roll(joined, 4, 0)
             edge_d[side, u] = pltpu.roll(depth, 5, 0)
+        relay(3 + side)
         return carry
 
     lax.fori_loop(0, 2, edges, 0)
@@ -360,7 +385,8 @@
             tensor = [
                 smooth_y([a + b for a, b in zip(c, d)]) for c, d in zip(pairs[u], pairs[u + 1])
             ]
-            w, m, t = parts(weight, u, span), parts(moment, u, span), parts(fix, u, span)
+            past = pl.ds(v0 + 1, STEP)
+            w, m, t = parts(weight, u, past), parts(moment, u, past), parts(fix, u, span)
             joined = [
                 jnp.where(rim, t[p], join(w[p], m[p], *(c[p] for c in tensor))) for p in range(4)
             ]
@@ -375,18 +401,10 @@
                 depth = joined[p] + 0.2 * (flux_x[p] - lanes(flux_x[p], -1) + flux_y[p] - above)
                 out[u, span, pl.ds(p, 8, stride=4), :] = jnp.where(outer, lanes(t[p], -63), depth)
 
-    def stored(k):
-        span = pl.ds(k * CHUNK, CHUNK)
-        return pltpu.make_async_copy(out.at[:, span], o_hbm.at[:, span], out_s.at[k])
-
     def chunk(k, carry):
-        @pl.when(k + 1 < CHUNKS)
+        @pl.when(jnp.logical_and(k >= 5 - AHEAD, k + AHEAD < CHUNKS))
         def _():
-            near_in(k + 1).wait_recv()
-
-            @pl.when(sends_far)
-            def _():
-                far(k + 1).start()
+            relay(k + AHEAD)
 
         @pl.when(has_far)
         def _():
@@ -397,7 +415,6 @@
             return c
 
         lax.fori_loop(0, CHUNK // STEP, inner, 0)
-        stored(k).start()
         return carry
 
     lax.fori_loop(0, CHUNKS, chunk, 0)
@@ -413,9 +430,6 @@
         mid_far.wait_send()
         for k in range(CHUNKS):
             far(k).wait_send()
-
-    for k in range(CHUNKS):
-        stored(k).wait()
 
 
 def local(nv, nc, light_field):
@@ -424,16 +438,15 @@
     return pl.pallas_call(
         functools.partial(kernel, nv, nc),
         out_shape=jax.ShapeDtypeStruct(block, F32),
-        in_specs=[pl.BlockSpec(memory_space=pl.ANY)],
-        out_specs=pl.BlockSpec(memory_space=pl.ANY),
+        in_specs=[pl.BlockSpec(memory_space=pltpu.HBM)],
+        out_specs=pl.BlockSpec(memory_space=pltpu.VMEM),
         scratch_shapes=[
             pltpu.VMEM(block, BF16),
             pltpu.VMEM(block, F32),
             pltpu.VMEM((2, *block), BF16),
             pltpu.VMEM((4, STEP, Y, X), F32),
-            pltpu.VMEM(block, F32),
-            pltpu.VMEM(block, F32),
-            pltpu.VMEM(block, F32),
+            pltpu.VMEM((ROWS, V + 1, Y, X), F32),
+            pltpu.VMEM((ROWS, V + 1, Y, X), F32),
             pltpu.VMEM(block, F32),
             pltpu.VMEM((16, PLANE), BF16),
             pltpu.VMEM((16, PLANE), BF16),
@@ -452,7 +465,6 @@
             dma((2,)),
             dma((2,)),
             dma((2,)),
-            dma((CHUNKS,)),
         ],
         compiler_params=pltpu.CompilerParams(
             collective_id=0, has_side_effects=True, vmem_limit_bytes=32 << 20

time: 47.2 us -> 28.6 us (0.61)
  the two profiles are of different devices: /device:TPU:4 before, /device:TPU:38 now
where the time goes in v2:
time: 28.6 us; the launch traced here: 28.5 us
  Pallas kernels  26.5 us (93%)
  local copies, waits for them, and re-layouts  2.01 us (7%)
    pallas_call x1, Pallas kernels, local(): pl.pallas_call(functools.partial(kernel, nv, nc), out_shape=jax.ShapeDtyp...  26.5 us
    unnamed x3, local copies, waits for them, and re-layouts  2.01 us

profile of v2, /device:TPU:38, one launch (start us, length us, event | category | flops | bytes accessed | tf_op | source)
XLA Modules:
  0.0 28.5 jit_solution(4887392873651469086)
XLA Ops:
  0.0 0.0 copy-start
  0.0 1.0 %copy-done = bf16[2,32,32,128]{3,2,1,0:T(8,128)(2,1)S(1)} copy-done((bf16[2,32,32,128]{3,2,1,0:T(8,128)(2,1)S(1)}, bf16[2,32,32,128]{3,2,1,0:T(8,128)(2,1)}, u32[]{:S(2)}) %copy-start) | copy-done | bytes 524312
  1.0 26.5 %shard_map.17 = f32[2,32,32,128]{3,2,1,0:T(8,128)S(1)} custom-call(bf16[2,32,32,128]{3,2,1,0:T(8,128)(2,1)S(1)} %copy-done), custom_call_target="tpu_custom_call" | custom-call | flops 60000000 | bytes 1600000 | tf_op jit(solution)/shard_map/pallas_call | solution.py:438
  27.5 1.0 %copy.3 = f32[2,32,32,128]{3,2,1,0:T(8,128)} copy(f32[2,32,32,128]{3,2,1,0:T(8,128)S(1)} %shard_map.17) | data formatting | bytes 2097152
Async XLA Ops:
  0.0 1.0 %copy-start = (bf16[2,32,32,128]{3,2,1,0:T(8,128)(2,1)S(1)}, bf16[2,32,32,128]{3,2,1,0:T(8,128)(2,1)}, u32[]{:S(2)}) copy-start(bf16[2,32,32,128]{3,2,1,0:T(8,128)(2,1)} %f_hbm.1) | copy-start | bytes 1572868

commit v3 on v2

--- a/solution.py
+++ b/solution.py
@@ -11,13 +11,14 @@
 F32 = jnp.float32
 BF16 = jnp.bfloat16
 ROWS, V, Y, X = 2, 32, 32, 128
-CHUNK = 4
+CHUNK = 2
 CHUNKS = V // CHUNK
 STEP = 4
 H_CHUNK = 8
 H_STEPS = V // H_CHUNK
-AHEAD = 3
-FIRST = 3
+FIRST = 2
+SECOND = 9
+EARLY = 3
 PLANE = V * Y
 
 
@@ -58,6 +59,7 @@
     weight,
     moment,
     fix,
+    slope,
     pack,
     pack_l,
     pack_r,
@@ -91,11 +93,51 @@
     sends_far = jnp.logical_and(vi != nv - 2, vi != 1)
 
     barrier = pltpu.get_barrier_semaphore()
-    for there in ((partner, cj), (behind, cj), (vi, left), (vi, right)):
+    has_left, has_right = cj > 0, cj < nc - 1
+
+    def greet(there):
         pl.semaphore_signal(barrier, inc=1, device_id=there, device_id_type=MESH)
+
+    greet((partner, cj))
+    for exists, there in ((has_far, (behind, cj)), (has_left, (vi, left)), (has_right, (vi, right))):
+
+        @pl.when(exists)
+        def _():
+            greet(there)
 
     load = pltpu.make_async_copy(f_hbm, fv, load_sem)
     load.start()
+
+    def remote(src, dst, s, r, there):
+        return pltpu.make_async_remote_copy(
+            src_ref=src, dst_ref=dst, send_sem=s, recv_sem=r, device_id=there, device_id_type=MESH
+        )
+
+    def near(k):
+        span = pl.ds(k * CHUNK, CHUNK)
+        return remote(f_hbm.at[:, span], got.at[odd, :, span], near_s.at[k], near_r.at[k], (partner, cj))
+
+    def near_in(k):
+        span = pl.ds(k * CHUNK, CHUNK)
+        return remote(f_hbm.at[:, span], got.at[even, :, span], near_s.at[k], near_r.at[k], (partner, cj))
+
+    def far(k):
+        span = pl.ds(k * CHUNK, CHUNK)
+        return remote(got.at[even, :, span], got.at[odd, :, span], far_s.at[k], far_r.at[k], (ahead, cj))
+
+    to_left = remote(pack, pack_r, pack_s.at[0], pack_rs.at[0], (vi, left))
+    to_right = remote(pack, pack_l, pack_s.at[1], pack_rs.at[1], (vi, right))
+
+    one = jnp.int32(1)
+    pl.semaphore_wait(
+        barrier,
+        one
+        + jnp.where(sends_far, 1, 0)
+        + jnp.where(has_left, 1, 0)
+        + jnp.where(has_right, 1, 0),
+    )
+    for k in range(FIRST):
+        near(k).start()
     load.wait()
 
     row8 = lax.broadcasted_iota(jnp.int32, (8, PLANE), 0)
@@ -112,30 +154,15 @@
         )
     pack[...] = packed.astype(BF16)
 
-    pl.semaphore_wait(barrier, 4)
-
-    def remote(src, dst, s, r, there):
-        return pltpu.make_async_remote_copy(
-            src_ref=src, dst_ref=dst, send_sem=s, recv_sem=r, device_id=there, device_id_type=MESH
-        )
-
-    def near(k):
-        span = pl.ds(k * CHUNK, CHUNK)
-        return remote(fv.at[:, span], got.at[odd, :, span], near_s.at[k], near_r.at[k], (partner, cj))
-
-    def near_in(k):
-        span = pl.ds(k * CHUNK, CHUNK)
-        return remote(fv.at[:, span], got.at[even, :, span], near_s.at[k], near_r.at[k], (partner, cj))
-
-    def far(k):
-        span = pl.ds(k * CHUNK, CHUNK)
-        return remote(got.at[even, :, span], got.at[odd, :, span], far_s.at[k], far_r.at[k], (ahead, cj))
-
-    to_left = remote(pack, pack_r, pack_s.at[0], pack_rs.at[0], (vi, left))
-    to_right = remote(pack, pack_l, pack_s.at[1], pack_rs.at[1], (vi, right))
-    to_left.start()
-    to_right.start()
-    for k in range(FIRST):
+    @pl.when(has_left)
+    def _():
+        to_left.start()
+
+    @pl.when(has_right)
+    def _():
+        to_right.start()
+
+    for k in range(FIRST, SECOND):
         near(k).start()
 
     @pl.when(at_top)
@@ -193,10 +220,26 @@
         return [c[H_CHUNK - 2] for c in now], [c[H_CHUNK - 1] for c in now]
 
     zeros = [jnp.zeros((Y, X), F32)] * 3
-    lax.fori_loop(0, H_STEPS, horizontal, (zeros, zeros))
-
-    to_left.wait_recv()
-    to_right.wait_recv()
+    lax.fori_loop(0, 2 * H_STEPS, horizontal, (zeros, zeros))
+
+    def relay(k):
+        near_in(k).wait_recv()
+
+        @pl.when(sends_far)
+        def _():
+            far(k).start()
+
+    for k in range(EARLY):
+        relay(k)
+
+    @pl.when(has_left)
+    def _():
+        to_right.wait_recv()
+
+    @pl.when(has_right)
+    def _():
+        to_left.wait_recv()
+
     first, final = cj == 0, cj == nc - 1
     own = pack[...].astype(F32)
     from_l = pack_l[...].astype(F32)
@@ -220,27 +263,102 @@
     mid_near_in = remote(mid, mids.at[even], mid_s.at[0], mid_r.at[0], (partner, cj))
     mid_far = remote(mids.at[even], mids.at[odd], mid_s.at[1], mid_r.at[1], (ahead, cj))
     mid_near.start()
-    for k in range(FIRST, CHUNKS):
+    for k in range(SECOND, CHUNKS):
         near(k).start()
 
-    def relay(k):
-        near_in(k).wait_recv()
-
-        @pl.when(sends_far)
+    lane = lax.broadcasted_iota(jnp.int32, (STEP, 8, X), 2)
+    sub = lax.broadcasted_iota(jnp.int32, (STEP, 8, X), 1)
+    rim = jnp.logical_or(lane < 2, lane >= X - 2)
+    outer = jnp.logical_or(lane == 0, lane == X - 1)
+
+    def parts(ref, *at):
+        return [ref[(*at, pl.ds(p, 8, stride=4), slice(None))] for p in range(4)]
+
+    def y_up(a, rest=0.0):
+        return a[1:] + [jnp.where(sub == 7, rest, pltpu.roll(a[0], 7, 1))]
+
+    def y_down(a):
+        return [jnp.where(sub == 0, 0.0, pltpu.roll(a[3], 1, 1))] + a[:3]
+
+    def smooth_y(a):
+        pair = [b + c for b, c in zip(a, y_down(a))]
+        return [b + c for b, c in zip(pair, y_up(pair, a[3]))]
+
+    def vertical(v0):
+        span = pl.ds(v0, STEP)
+        for slot in range(2):
+            for u in range(ROWS):
+                wide[2 * slot + u] = got[slot, u, span].astype(F32)
+        every = slice(None)
+        field = (
+            [parts(wide, 0, every), parts(wide, 1, every)]
+            + [parts(full, u, span) for u in range(ROWS)]
+            + [parts(wide, 2, every), parts(wide, 3, every)]
+        )
+        comps = []
+        for r in range(1, 5):
+            grad_u = [a - b for a, b in zip(field[r + 1], field[r - 1])]
+            grad_y = [a - b for a, b in zip(y_up(field[r]), y_down(field[r]))]
+            comps.append(
+                [
+                    [a * b for a, b in zip(g, h)]
+                    for g, h in ((grad_u, grad_u), (grad_u, grad_y), (grad_y, grad_y))
+                ]
+            )
+        pairs = [
+            [[a + b for a, b in zip(c, d)] for c, d in zip(comps[r], comps[r + 1])] for r in range(3)
+        ]
+        for u in range(ROWS):
+            tensor = [
+                smooth_y([a + b for a, b in zip(c, d)]) for c, d in zip(pairs[u], pairs[u + 1])
+            ]
+            past = pl.ds(v0 + 1, STEP)
+            w, m = parts(weight, u, past), parts(moment, u, past)
+            for p in range(4):
+                slope[u, span, p] = join(w[p], m[p], *(c[p] for c in tensor))
+
+    def variation(v0):
+        span = pl.ds(v0, STEP)
+        for u in range(ROWS):
+            t = parts(fix, u, span)
+            joined = [jnp.where(rim, t[p], slope[u, span, p]) for p in range(4)]
+            flux_x, flux_y = [], []
+            for here, below in zip(joined, y_up(joined)):
+                step_x = lanes(here, 1) - here
+                step_y = below - here
+                scale = lax.rsqrt(step_x * step_x + step_y * step_y + 1.0)
+                flux_x.append(step_x * scale)
+                flux_y.append(step_y * scale)
+            for p, above in enumerate(y_down(flux_y)):
+                depth = joined[p] + 0.2 * (flux_x[p] - lanes(flux_x[p], -1) + flux_y[p] - above)
+                out[u, span, pl.ds(p, 8, stride=4), :] = jnp.where(outer, lanes(t[p], -63), depth)
+
+    for k in range(EARLY, EARLY + 2):
+        relay(k)
+
+    def arrived(g):
+        @pl.when(has_far)
         def _():
-            far(k).start()
-
-    lax.fori_loop(H_STEPS, 2 * H_STEPS, horizontal, (zeros, zeros))
-
-    relay(0)
-    relay(1)
-    mid_near_in.wait_recv()
-
-    @pl.when(sends_far)
-    def _():
-        mid_far.start()
-
-    relay(2)
+            far(2 * g).wait_recv()
+            far(2 * g + 1).wait_recv()
+
+    def start(g, carry):
+        relay(2 * g + EARLY + 2)
+        relay(2 * g + EARLY + 3)
+
+        @pl.when(g == 1)
+        def _():
+            mid_near_in.wait_recv()
+
+            @pl.when(sends_far)
+            def _():
+                mid_far.start()
+
+        arrived(g)
+        vertical(g * STEP)
+        return carry
+
+    lax.fori_loop(0, 4, start, 0)
 
     @pl.when(has_far)
     def _():
@@ -313,7 +431,7 @@
             depth = joined + 0.2 * (flux_x - cols_by(flux_x, -1) + flux_y - y_by(flux_y, -1))
             edge_j[side, u] = pltpu.roll(joined, 4, 0)
             edge_d[side, u] = pltpu.roll(depth, 5, 0)
-        relay(3 + side)
+        relay(EARLY + 10 + side)
         return carry
 
     lax.fori_loop(0, 2, edges, 0)
@@ -339,88 +457,26 @@
 
     lax.fori_loop(0, 2, spread_out, 0)
 
-    lane = lax.broadcasted_iota(jnp.int32, (STEP, 8, X), 2)
-    sub = lax.broadcasted_iota(jnp.int32, (STEP, 8, X), 1)
-    rim = jnp.logical_or(lane < 2, lane >= X - 2)
-    outer = jnp.logical_or(lane == 0, lane == X - 1)
-
-    def parts(ref, *at):
-        return [ref[(*at, pl.ds(p, 8, stride=4), slice(None))] for p in range(4)]
-
-    def y_up(a, rest=0.0):
-        return a[1:] + [jnp.where(sub == 7, rest, pltpu.roll(a[0], 7, 1))]
-
-    def y_down(a):
-        return [jnp.where(sub == 0, 0.0, pltpu.roll(a[3], 1, 1))] + a[:3]
-
-    def smooth_y(a):
-        pair = [b + c for b, c in zip(a, y_down(a))]
-        return [b + c for b, c in zip(pair, y_up(pair, a[3]))]
-
-    def vertical(v0):
-        span = pl.ds(v0, STEP)
-        for slot in range(2):
-            for u in range(ROWS):
-                wide[2 * slot + u] = got[slot, u, span].astype(F32)
-        every = slice(None)
-        field = (
-            [parts(wide, 0, every), parts(wide, 1, every)]
-            + [parts(full, u, span) for u in range(ROWS)]
-            + [parts(wide, 2, every), parts(wide, 3, every)]
-        )
-        comps = []
-        for r in range(1, 5):
-            grad_u = [a - b for a, b in zip(field[r + 1], field[r - 1])]
-            grad_y = [a - b for a, b in zip(y_up(field[r]), y_down(field[r]))]
-            comps.append(
-                [
-                    [a * b for a, b in zip(g, h)]
-                    for g, h in ((grad_u, grad_u), (grad_u, grad_y), (grad_y, grad_y))
-                ]
-            )
-        pairs = [
-            [[a + b for a, b in zip(c, d)] for c, d in zip(comps[r], comps[r + 1])] for r in range(3)
-        ]
-        for u in range(ROWS):
-            tensor = [
-                smooth_y([a + b for a, b in zip(c, d)]) for c, d in zip(pairs[u], pairs[u + 1])
-            ]
-            past = pl.ds(v0 + 1, STEP)
-            w, m, t = parts(weight, u, past), parts(moment, u, past), parts(fix, u, span)
-            joined = [
-                jnp.where(rim, t[p], join(w[p], m[p], *(c[p] for c in tensor))) for p in range(4)
-            ]
-            flux_x, flux_y = [], []
-            for here, below in zip(joined, y_up(joined)):
-                step_x = lanes(here, 1) - here
-                step_y = below - here
-                scale = lax.rsqrt(step_x * step_x + step_y * step_y + 1.0)
-                flux_x.append(step_x * scale)
-                flux_y.append(step_y * scale)
-            for p, above in enumerate(y_down(flux_y)):
-                depth = joined[p] + 0.2 * (flux_x[p] - lanes(flux_x[p], -1) + flux_y[p] - above)
-                out[u, span, pl.ds(p, 8, stride=4), :] = jnp.where(outer, lanes(t[p], -63), depth)
-
-    def chunk(k, carry):
-        @pl.when(jnp.logical_and(k >= 5 - AHEAD, k + AHEAD < CHUNKS))
-        def _():
-            relay(k + AHEAD)
-
-        @pl.when(has_far)
-        def _():
-            far(k).wait_recv()
-
-        def inner(i, c):
-            vertical(k * CHUNK + i * STEP)
-            return c
-
-        lax.fori_loop(0, CHUNK // STEP, inner, 0)
+    for k in range(EARLY + 12, CHUNKS):
+        relay(k)
+
+    def finish(i, carry):
+        arrived(4 + i)
+        vertical((4 + i) * STEP)
+        variation(2 * i * STEP)
+        variation((2 * i + 1) * STEP)
         return carry
 
-    lax.fori_loop(0, CHUNKS, chunk, 0)
-
-    to_left.wait_send()
-    to_right.wait_send()
+    lax.fori_loop(0, 4, finish, 0)
+
+    @pl.when(has_left)
+    def _():
+        to_left.wait_send()
+
+    @pl.when(has_right)
+    def _():
+        to_right.wait_send()
+
     mid_near.wait_send()
     for k in range(CHUNKS):
         near(k).wait_send()
@@ -438,7 +494,7 @@
     return pl.pallas_call(
         functools.partial(kernel, nv, nc),
         out_shape=jax.ShapeDtypeStruct(block, F32),
-        in_specs=[pl.BlockSpec(memory_space=pltpu.HBM)],
+        in_specs=[pl.BlockSpec(memory_space=pl.ANY)],
         out_specs=pl.BlockSpec(memory_space=pltpu.VMEM),
         scratch_shapes=[
             pltpu.VMEM(block, BF16),
@@ -448,6 +504,7 @@
             pltpu.VMEM((ROWS, V + 1, Y, X), F32),
             pltpu.VMEM((ROWS, V + 1, Y, X), F32),
             pltpu.VMEM(block, F32),
+            pltpu.VMEM((ROWS, V, 4, 8, X), F32),
             pltpu.VMEM((16, PLANE), BF16),
             pltpu.VMEM((16, PLANE), BF16),
             pltpu.VMEM((16, PLANE), BF16),
@@ -470,7 +527,7 @@
             collective_id=0, has_side_effects=True, vmem_limit_bytes=32 << 20
         ),
         cost_estimate=pl.CostEstimate(flops=60_000_000, bytes_accessed=1_600_000, transcendentals=800_000),
-    )(light_field)
+    )(pltpu.with_memory_space_constraint(light_field, pltpu.HBM))
 
 
 def solution(mesh):

time: 28.6 us -> 26.5 us (0.927)
  the two profiles are of different devices: /device:TPU:38 before, /device:TPU:70 now
where the time goes in v3:
time: 26.5 us; the launch traced here: 26.3 us
  Pallas kernels  25.4 us (96%)
  local copies, waits for them, and re-layouts  0.97 us (4%)
    pallas_call x1, Pallas kernels, local(): pl.pallas_call(functools.partial(kernel, nv, nc), out_shape=jax.ShapeDtyp...  25.4 us
    unnamed x1, local copies, waits for them, and re-layouts  0.97 us

profile of v3, /device:TPU:70, one launch (start us, length us, event | category | flops | bytes accessed | tf_op | source)
XLA Modules:
  0.0 26.3 jit_solution(3307163997174073492)
XLA Ops:
  0.0 25.4 %shard_map.17 = f32[2,32,32,128]{3,2,1,0:T(8,128)S(1)} custom-call(bf16[2,32,32,128]{3,2,1,0:T(8,128)(2,1)} %f_hbm.1), custom_call_target="tpu_custom_call" | custom-call | flops 60000000 | bytes 1600000 | tf_op jit(solution)/shard_map/pallas_call | solution.py:494
  25.4 1.0 %copy.3 = f32[2,32,32,128]{3,2,1,0:T(8,128)} copy(f32[2,32,32,128]{3,2,1,0:T(8,128)S(1)} %shard_map.17) | data formatting | bytes 2097152

commit v4 on v3

--- a/solution.py
+++ b/solution.py
@@ -16,9 +16,7 @@
 STEP = 4
 H_CHUNK = 8
 H_STEPS = V // H_CHUNK
-FIRST = 2
-SECOND = 9
-EARLY = 3
+FIRST = 6
 PLANE = V * Y
 
 
@@ -128,6 +126,22 @@
     to_left = remote(pack, pack_r, pack_s.at[0], pack_rs.at[0], (vi, left))
     to_right = remote(pack, pack_l, pack_s.at[1], pack_rs.at[1], (vi, right))
 
+    load.wait()
+
+    row8 = lax.broadcasted_iota(jnp.int32, (8, PLANE), 0)
+    row16 = lax.broadcasted_iota(jnp.int32, (16, X), 0)
+    lane16 = lax.broadcasted_iota(jnp.int32, (16, X), 1)
+    r8 = lax.rem(row16, 8)
+    wanted = jnp.where(r8 < 4, r8 + (X - 4), r8 - 4)
+
+    packed = jnp.zeros((16, PLANE), F32)
+    for u in range(ROWS):
+        pick = jnp.where(jnp.logical_and(lane16 == wanted, row16 // 8 == u), 1.0, 0.0).astype(BF16)
+        packed = packed + lax.dot_general(
+            pick, fv[u].reshape(PLANE, X), (((1,), (1,)), ((), ())), preferred_element_type=F32
+        )
+    pack[...] = packed.astype(BF16)
+
     one = jnp.int32(1)
     pl.semaphore_wait(
         barrier,
@@ -136,33 +150,15 @@
         + jnp.where(has_left, 1, 0)
         + jnp.where(has_right, 1, 0),
     )
+    @pl.when(has_left)
+    def _():
+        to_left.start()
+
+    @pl.when(has_right)
+    def _():
+        to_right.start()
+
     for k in range(FIRST):
-        near(k).start()
-    load.wait()
-
-    row8 = lax.broadcasted_iota(jnp.int32, (8, PLANE), 0)
-    row16 = lax.broadcasted_iota(jnp.int32, (16, X), 0)
-    lane16 = lax.broadcasted_iota(jnp.int32, (16, X), 1)
-    r8 = lax.rem(row16, 8)
-    wanted = jnp.where(r8 < 4, r8 + (X - 4), r8 - 4)
-
-    packed = jnp.zeros((16, PLANE), F32)
-    for u in range(ROWS):
-        pick = jnp.where(jnp.logical_and(lane16 == wanted, row16 // 8 == u), 1.0, 0.0).astype(BF16)
-        packed = packed + lax.dot_general(
-            pick, fv[u].reshape(PLANE, X), (((1,), (1,)), ((), ())), preferred_element_type=F32
-        )
-    pack[...] = packed.astype(BF16)
-
-    @pl.when(has_left)
-    def _():
-        to_left.start()
-
-    @pl.when(has_right)
-    def _():
-        to_right.start()
-
-    for k in range(FIRST, SECOND):
         near(k).start()
 
     @pl.when(at_top)
@@ -221,16 +217,6 @@
 
     zeros = [jnp.zeros((Y, X), F32)] * 3
     lax.fori_loop(0, 2 * H_STEPS, horizontal, (zeros, zeros))
-
-    def relay(k):
-        near_in(k).wait_recv()
-
-        @pl.when(sends_far)
-        def _():
-            far(k).start()
-
-    for k in range(EARLY):
-        relay(k)
 
     @pl.when(has_left)
     def _():
@@ -263,8 +249,17 @@
     mid_near_in = remote(mid, mids.at[even], mid_s.at[0], mid_r.at[0], (partner, cj))
     mid_far = remote(mids.at[even], mids.at[odd], mid_s.at[1], mid_r.at[1], (ahead, cj))
     mid_near.start()
-    for k in range(SECOND, CHUNKS):
+    for k in range(FIRST, CHUNKS):
         near(k).start()
+
+    def relay(k):
+        near_in(k).wait_recv()
+
+        @pl.when(sends_far)
+        def _():
+            far(k).start()
+
+    relay(0)
 
     lane = lax.broadcasted_iota(jnp.int32, (STEP, 8, X), 2)
     sub = lax.broadcasted_iota(jnp.int32, (STEP, 8, X), 1)
@@ -333,8 +328,46 @@
                 depth = joined[p] + 0.2 * (flux_x[p] - lanes(flux_x[p], -1) + flux_y[p] - above)
                 out[u, span, pl.ds(p, 8, stride=4), :] = jnp.where(outer, lanes(t[p], -63), depth)
 
-    for k in range(EARLY, EARLY + 2):
+    place = lax.broadcasted_iota(jnp.int32, (8, PLANE), 1)
+    y_at = lax.rem(place, Y)
+
+    def cols_by(a, k):
+        return pltpu.roll(a, (-k) % 8, 0)
+
+    def y_by(a, k):
+        return jnp.where(y_at == (Y - 1 if k > 0 else 0), 0.0, pltpu.roll(a, (-k) % PLANE, 1))
+
+    def v_by(a, k):
+        return jnp.where(
+            place >= PLANE - Y if k > 0 else place < Y, 0.0, pltpu.roll(a, (-k * Y) % PLANE, 1)
+        )
+
+    def smooth_by(by, a):
+        return by(a, -1) + (a + a) + by(a, 1)
+
+    def edges_h(side, carry):
+        for u in range(ROWS):
+            f = edge[side, 2 + u]
+            grad_v = v_by(f, 1) - v_by(f, -1)
+            grad_x = cols_by(f, 1) - cols_by(f, -1)
+            w, m = weighted(
+                *(
+                    smooth_by(v_by, smooth_by(cols_by, c))
+                    for c in (grad_v * grad_v, grad_v * grad_x, grad_x * grad_x)
+                )
+            )
+            edge_j[side, u] = w
+            edge_d[side, u] = m
+        return carry
+
+    lax.fori_loop(0, 2, edges_h, 0)
+    for k in range(1, 6):
         relay(k)
+    mid_near_in.wait_recv()
+
+    @pl.when(sends_far)
+    def _():
+        mid_far.start()
 
     def arrived(g):
         @pl.when(has_far)
@@ -343,22 +376,13 @@
             far(2 * g + 1).wait_recv()
 
     def start(g, carry):
-        relay(2 * g + EARLY + 2)
-        relay(2 * g + EARLY + 3)
-
-        @pl.when(g == 1)
-        def _():
-            mid_near_in.wait_recv()
-
-            @pl.when(sends_far)
-            def _():
-                mid_far.start()
-
+        relay(2 * g + 6)
+        relay(2 * g + 7)
         arrived(g)
         vertical(g * STEP)
         return carry
 
-    lax.fori_loop(0, 4, start, 0)
+    lax.fori_loop(0, 2, start, 0)
 
     @pl.when(has_far)
     def _():
@@ -382,23 +406,6 @@
         for side in range(2):
             edge[side, 4] = jnp.zeros((8, PLANE), F32)
             edge[side, 5] = edge[side, 3]
-
-    place = lax.broadcasted_iota(jnp.int32, (8, PLANE), 1)
-    y_at = lax.rem(place, Y)
-
-    def cols_by(a, k):
-        return pltpu.roll(a, (-k) % 8, 0)
-
-    def y_by(a, k):
-        return jnp.where(y_at == (Y - 1 if k > 0 else 0), 0.0, pltpu.roll(a, (-k) % PLANE, 1))
-
-    def v_by(a, k):
-        return jnp.where(
-            place >= PLANE - Y if k > 0 else place < Y, 0.0, pltpu.roll(a, (-k * Y) % PLANE, 1)
-        )
-
-    def smooth_by(by, a):
-        return by(a, -1) + (a + a) + by(a, 1)
 
     def edges(side, carry):
         j_below = jnp.where(jnp.logical_and(final, side == 1), 4, 8)
@@ -410,15 +417,7 @@
             grad_y = y_by(tiles[r], 1) - y_by(tiles[r], -1)
             comps.append((grad_u * grad_u, grad_u * grad_y, grad_y * grad_y))
         for u in range(ROWS):
-            f = tiles[2 + u]
-            grad_v = v_by(f, 1) - v_by(f, -1)
-            grad_x = cols_by(f, 1) - cols_by(f, -1)
-            w, m = weighted(
-                *(
-                    smooth_by(v_by, smooth_by(cols_by, c))
-                    for c in (grad_v * grad_v, grad_v * grad_x, grad_x * grad_x)
-                )
-            )
+            w, m = edge_j[side, u], edge_d[side, u]
             tensor = [
                 smooth_by(y_by, a + (b + b) + c) for a, b, c in zip(comps[u], comps[u + 1], comps[u + 2])
             ]
@@ -431,7 +430,7 @@
             depth = joined + 0.2 * (flux_x - cols_by(flux_x, -1) + flux_y - y_by(flux_y, -1))
             edge_j[side, u] = pltpu.roll(joined, 4, 0)
             edge_d[side, u] = pltpu.roll(depth, 5, 0)
-        relay(EARLY + 10 + side)
+        relay(10 + side)
         return carry
 
     lax.fori_loop(0, 2, edges, 0)
@@ -457,17 +456,24 @@
 
     lax.fori_loop(0, 2, spread_out, 0)
 
-    for k in range(EARLY + 12, CHUNKS):
-        relay(k)
-
-    def finish(i, carry):
-        arrived(4 + i)
-        vertical((4 + i) * STEP)
-        variation(2 * i * STEP)
-        variation((2 * i + 1) * STEP)
+    def finish(g, carry):
+        for k in range(2):
+
+            @pl.when(2 * g + k + 8 < CHUNKS)
+            def _():
+                relay(2 * g + k + 8)
+
+        def varied(i, c):
+            variation(i * STEP)
+            return c
+
+        lax.fori_loop(jnp.where(g < 4, g - 2, g - 1), jnp.where(g == 2, 1, g), varied, 0)
+        arrived(g)
+        vertical(g * STEP)
         return carry
 
-    lax.fori_loop(0, 4, finish, 0)
+    lax.fori_loop(2, V // STEP, finish, 0)
+    variation(V - STEP)
 
     @pl.when(has_left)
     def _():

time: 26.5 us -> 24.4 us (0.921)
  Pallas kernels: 25.4 us -> 23.3 us
    pallas_call x1, Pallas kernels: 25.4 us -> 23.3 us  [local(): pl.pallas_call(functools.partial(kernel, nv, nc), out_shape=jax.ShapeDtyp...]
where the time goes in v4:
time: 24.4 us; the launch traced here: 24.3 us
  Pallas kernels  23.3 us (95%)
  local copies, waits for them, and re-layouts  0.97 us (4%)
    pallas_call x1, Pallas kernels, local(): pl.pallas_call(functools.partial(kernel, nv, nc), out_shape=jax.ShapeDtyp...  23.3 us
    unnamed x1, local copies, waits for them, and re-layouts  0.97 us

profile of v4, /device:TPU:70, one launch (start us, length us, event | category | flops | bytes accessed | tf_op | source)
XLA Modules:
  0.0 24.3 jit_solution(16101359419856914685)
XLA Ops:
  0.0 23.3 %shard_map.17 = f32[2,32,32,128]{3,2,1,0:T(8,128)S(1)} custom-call(bf16[2,32,32,128]{3,2,1,0:T(8,128)(2,1)} %f_hbm.1), custom_call_target="tpu_custom_call" | custom-call | flops 60000000 | bytes 1600000 | tf_op jit(solution)/shard_map/pallas_call | solution.py:500
  23.3 1.0 %copy.3 = f32[2,32,32,128]{3,2,1,0:T(8,128)} copy(f32[2,32,32,128]{3,2,1,0:T(8,128)S(1)} %shard_map.17) | data formatting | bytes 2097152

commit v5 on v4

--- a/solution.py
+++ b/solution.py
@@ -16,7 +16,9 @@
 STEP = 4
 H_CHUNK = 8
 H_STEPS = V // H_CHUNK
+BEFORE = 3
 FIRST = 6
+FLIGHT = 8
 PLANE = V * Y
 
 
@@ -59,10 +61,11 @@
     fix,
     slope,
     pack,
+    pack_out,
     pack_l,
     pack_r,
-    mid,
-    mids,
+    own_cols,
+    cols_in,
     edge,
     edge_j,
     edge_d,
@@ -73,8 +76,8 @@
     far_r,
     pack_s,
     pack_rs,
-    mid_s,
-    mid_r,
+    cols_s,
+    cols_r,
 ):
     vi = lax.axis_index("views")
     cj = lax.axis_index("cols")
@@ -113,18 +116,18 @@
 
     def near(k):
         span = pl.ds(k * CHUNK, CHUNK)
-        return remote(f_hbm.at[:, span], got.at[odd, :, span], near_s.at[k], near_r.at[k], (partner, cj))
+        return remote(f_hbm.at[:, span], got.at[odd, :, span], near_s, near_r.at[k], (partner, cj))
 
     def near_in(k):
         span = pl.ds(k * CHUNK, CHUNK)
-        return remote(f_hbm.at[:, span], got.at[even, :, span], near_s.at[k], near_r.at[k], (partner, cj))
+        return remote(f_hbm.at[:, span], got.at[even, :, span], near_s, near_r.at[k], (partner, cj))
 
     def far(k):
         span = pl.ds(k * CHUNK, CHUNK)
-        return remote(got.at[even, :, span], got.at[odd, :, span], far_s.at[k], far_r.at[k], (ahead, cj))
-
-    to_left = remote(pack, pack_r, pack_s.at[0], pack_rs.at[0], (vi, left))
-    to_right = remote(pack, pack_l, pack_s.at[1], pack_rs.at[1], (vi, right))
+        return remote(got.at[even, :, span], got.at[odd, :, span], far_s, far_r.at[k // 2], (ahead, cj))
+
+    to_left = remote(pack_out.at[0], pack_r, pack_s.at[0], pack_rs.at[0], (vi, left))
+    to_right = remote(pack_out.at[1], pack_l, pack_s.at[1], pack_rs.at[1], (vi, right))
 
     load.wait()
 
@@ -141,6 +144,18 @@
             pick, fv[u].reshape(PLANE, X), (((1,), (1,)), ((), ())), preferred_element_type=F32
         )
     pack[...] = packed.astype(BF16)
+
+    def folded(a):
+        return jnp.concatenate([a[:, : PLANE // 2], a[:, PLANE // 2 :]], axis=0).astype(BF16)
+
+    def unfolded(a):
+        a = a.astype(F32)
+        return jnp.concatenate([a[:8], a[8:]], axis=1)
+
+    pack_out[0] = folded(jnp.where(row8 < 4, pltpu.roll(packed[:8], 4, 0), packed[8:]))
+    pack_out[1] = folded(jnp.where(row8 < 4, packed[:8], pltpu.roll(packed[8:], 4, 0)))
+    four = jnp.where(row8 < 4, pltpu.roll(packed[:8], 6, 0), pltpu.roll(packed[8:], 2, 0))
+    own_cols[...] = folded(four)
 
     one = jnp.int32(1)
     pl.semaphore_wait(
@@ -158,8 +173,39 @@
     def _():
         to_right.start()
 
+    cols_near = remote(own_cols, cols_in.at[1, odd], cols_s.at[0], cols_r.at[0], (partner, cj))
+    cols_far = remote(cols_in.at[1, even], cols_in.at[1, odd], cols_s.at[1], cols_r.at[1], (ahead, cj))
+    cols_near.start()
     for k in range(FIRST):
         near(k).start()
+
+    held = jnp.logical_or(cj == nc // 2 - 1, cj == nc // 2)
+
+    @pl.when(jnp.logical_not(held))
+    def _():
+        for k in range(FIRST, CHUNKS):
+            near(k).start()
+
+    def passed(far_too, slot):
+        return (
+            remote(
+                cols_in.at[1, slot],
+                cols_in.at[2, slot],
+                cols_s.at[2 + far_too],
+                cols_r.at[2 + far_too],
+                (vi, left),
+            ),
+            remote(
+                cols_in.at[1, slot],
+                cols_in.at[0, slot],
+                cols_s.at[4 + far_too],
+                cols_r.at[4 + far_too],
+                (vi, right),
+            ),
+        )
+
+    near_left, near_right = passed(0, even)
+    far_left, far_right = passed(1, odd)
 
     @pl.when(at_top)
     def _():
@@ -218,48 +264,36 @@
     zeros = [jnp.zeros((Y, X), F32)] * 3
     lax.fori_loop(0, 2 * H_STEPS, horizontal, (zeros, zeros))
 
+    cols_near.wait_recv()
+
+    @pl.when(sends_far)
+    def _():
+        cols_far.start()
+
     @pl.when(has_left)
     def _():
-        to_right.wait_recv()
+        near_left.start()
 
     @pl.when(has_right)
     def _():
-        to_left.wait_recv()
-
-    first, final = cj == 0, cj == nc - 1
-    own = pack[...].astype(F32)
-    from_l = pack_l[...].astype(F32)
-    from_r = pack_r[...].astype(F32)
-    mixed = []
-    for u in range(ROWS):
-        mine = own[8 * u : 8 * u + 8]
-        l_in = from_l[8 * u : 8 * u + 8]
-        r_in = from_r[8 * u : 8 * u + 8]
-        flip_l = jnp.where(row8 == 2, pltpu.roll(mine, 6, 0), 0.0)
-        flip_r = jnp.where(row8 == 5, pltpu.roll(mine, 2, 0), 0.0)
-        l_in = jnp.where(first, flip_l, l_in)
-        r_in = jnp.where(final, flip_r, r_in)
-        e_l = jnp.where(row8 < 4, l_in, mine)
-        e_r = jnp.where(row8 < 4, mine, r_in)
-        edge[0, 2 + u] = e_l
-        edge[1, 2 + u] = e_r
-        mixed.append(jnp.where(jnp.logical_and(row8 >= 2, row8 < 6), e_l, pltpu.roll(e_r, 4, 0)))
-    mid[...] = jnp.concatenate(mixed, axis=0).astype(BF16)
-    mid_near = remote(mid, mids.at[odd], mid_s.at[0], mid_r.at[0], (partner, cj))
-    mid_near_in = remote(mid, mids.at[even], mid_s.at[0], mid_r.at[0], (partner, cj))
-    mid_far = remote(mids.at[even], mids.at[odd], mid_s.at[1], mid_r.at[1], (ahead, cj))
-    mid_near.start()
-    for k in range(FIRST, CHUNKS):
-        near(k).start()
+        near_right.start()
+
+    @pl.when(held)
+    def _():
+        for k in range(FIRST, FLIGHT):
+            near(k).start()
 
     def relay(k):
         near_in(k).wait_recv()
 
+        @pl.when(jnp.logical_and(held, k + FLIGHT < CHUNKS))
+        def _():
+            near(k + FLIGHT).start()
+
         @pl.when(sends_far)
         def _():
             far(k).start()
 
-    relay(0)
 
     lane = lax.broadcasted_iota(jnp.int32, (STEP, 8, X), 2)
     sub = lax.broadcasted_iota(jnp.int32, (STEP, 8, X), 1)
@@ -345,6 +379,35 @@
     def smooth_by(by, a):
         return by(a, -1) + (a + a) + by(a, 1)
 
+    relay(0)
+    relay(1)
+    relay(2)
+
+    @pl.when(has_left)
+    def _():
+        to_right.wait_recv()
+
+    @pl.when(has_right)
+    def _():
+        to_left.wait_recv()
+
+    first, final = cj == 0, cj == nc - 1
+    own = pack[...].astype(F32)
+    from_l = unfolded(pack_l[...])
+    from_r = unfolded(pack_r[...])
+    for u in range(ROWS):
+        mine = own[8 * u : 8 * u + 8]
+        l_in = pltpu.roll(from_l, 4, 0) if u else from_l
+        r_in = from_r if u else pltpu.roll(from_r, 4, 0)
+        flip_l = jnp.where(row8 == 2, pltpu.roll(mine, 6, 0), 0.0)
+        flip_r = jnp.where(row8 == 5, pltpu.roll(mine, 2, 0), 0.0)
+        l_in = jnp.where(first, flip_l, l_in)
+        r_in = jnp.where(final, flip_r, r_in)
+        e_l = jnp.where(row8 < 4, l_in, mine)
+        e_r = jnp.where(row8 < 4, mine, r_in)
+        edge[0, 2 + u] = e_l
+        edge[1, 2 + u] = e_r
+
     def edges_h(side, carry):
         for u in range(ROWS):
             f = edge[side, 2 + u]
@@ -358,22 +421,32 @@
             )
             edge_j[side, u] = w
             edge_d[side, u] = m
+        relay(3 + side)
         return carry
 
     lax.fori_loop(0, 2, edges_h, 0)
-    for k in range(1, 6):
-        relay(k)
-    mid_near_in.wait_recv()
-
-    @pl.when(sends_far)
-    def _():
-        mid_far.start()
+
+    @pl.when(has_far)
+    def _():
+        cols_far.wait_recv()
+
+        @pl.when(has_left)
+        def _():
+            far_left.start()
+
+        @pl.when(has_right)
+        def _():
+            far_right.start()
+
+    relay(5)
 
     def arrived(g):
         @pl.when(has_far)
         def _():
-            far(2 * g).wait_recv()
-            far(2 * g + 1).wait_recv()
+            both = pl.ds(g * STEP, STEP)
+            remote(
+                got.at[even, :, both], got.at[odd, :, both], far_s, far_r.at[g], (ahead, cj)
+            ).wait_recv()
 
     def start(g, carry):
         relay(2 * g + 6)
@@ -382,18 +455,33 @@
         vertical(g * STEP)
         return carry
 
-    lax.fori_loop(0, 2, start, 0)
-
-    @pl.when(has_far)
-    def _():
-        mid_far.wait_recv()
+    lax.fori_loop(0, BEFORE, start, 0)
+
+    @pl.when(has_left)
+    def _():
+        near_right.wait_recv()
+
+        @pl.when(has_far)
+        def _():
+            far_right.wait_recv()
+
+    @pl.when(has_right)
+    def _():
+        near_left.wait_recv()
+
+        @pl.when(has_far)
+        def _():
+            far_left.wait_recv()
 
     for slot in range(2):
-        rows_in = mids[slot].astype(F32)
+        from_l, here, from_r = (
+            unfolded(cols_in[origin, slot]) for origin in range(3)
+        )
         for u in range(ROWS):
-            tile = rows_in[8 * u : 8 * u + 8]
-            edge[0, 4 * slot + u] = tile
-            edge[1, 4 * slot + u] = pltpu.roll(tile, 4, 0)
+            with_l = jnp.where(row8 == 4 * u + 1, from_l, here)
+            with_r = jnp.where(row8 == 4 * u + 2, from_r, here)
+            edge[0, 4 * slot + u] = pltpu.roll(with_l, 2 + 4 * u, 0)
+            edge[1, 4 * slot + u] = pltpu.roll(with_r, 2 + 4 * u, 0)
 
     @pl.when(at_top)
     def _():
@@ -430,7 +518,7 @@
             depth = joined + 0.2 * (flux_x - cols_by(flux_x, -1) + flux_y - y_by(flux_y, -1))
             edge_j[side, u] = pltpu.roll(joined, 4, 0)
             edge_d[side, u] = pltpu.roll(depth, 5, 0)
-        relay(10 + side)
+        relay(2 * BEFORE + 6 + side)
         return carry
 
     lax.fori_loop(0, 2, edges, 0)
@@ -467,31 +555,39 @@
             variation(i * STEP)
             return c
 
-        lax.fori_loop(jnp.where(g < 4, g - 2, g - 1), jnp.where(g == 2, 1, g), varied, 0)
+        lax.fori_loop(jnp.where(g == BEFORE, 0, g - 1), g, varied, 0)
         arrived(g)
         vertical(g * STEP)
         return carry
 
-    lax.fori_loop(2, V // STEP, finish, 0)
+    lax.fori_loop(BEFORE, V // STEP, finish, 0)
     variation(V - STEP)
 
     @pl.when(has_left)
     def _():
         to_left.wait_send()
+        near_left.wait_send()
 
     @pl.when(has_right)
     def _():
         to_right.wait_send()
-
-    mid_near.wait_send()
-    for k in range(CHUNKS):
-        near(k).wait_send()
+        near_right.wait_send()
+
+    @pl.when(jnp.logical_and(has_left, has_far))
+    def _():
+        far_left.wait_send()
+
+    @pl.when(jnp.logical_and(has_right, has_far))
+    def _():
+        far_right.wait_send()
+
+    cols_near.wait_send()
+    remote(f_hbm, got.at[odd], near_s, near_r.at[0], (partner, cj)).wait_send()
 
     @pl.when(sends_far)
     def _():
-        mid_far.wait_send()
-        for k in range(CHUNKS):
-            far(k).wait_send()
+        cols_far.wait_send()
+        remote(got.at[even], got.at[odd], far_s, far_r.at[0], (ahead, cj)).wait_send()
 
 
 def local(nv, nc, light_field):
@@ -512,22 +608,23 @@
             pltpu.VMEM(block, F32),
             pltpu.VMEM((ROWS, V, 4, 8, X), F32),
             pltpu.VMEM((16, PLANE), BF16),
-            pltpu.VMEM((16, PLANE), BF16),
-            pltpu.VMEM((16, PLANE), BF16),
-            pltpu.VMEM((16, PLANE), BF16),
-            pltpu.VMEM((2, 16, PLANE), BF16),
+            pltpu.VMEM((2, 16, PLANE // 2), BF16),
+            pltpu.VMEM((16, PLANE // 2), BF16),
+            pltpu.VMEM((16, PLANE // 2), BF16),
+            pltpu.VMEM((16, PLANE // 2), BF16),
+            pltpu.VMEM((3, 2, 16, PLANE // 2), BF16),
             pltpu.VMEM((2, 6, 8, PLANE), F32),
             pltpu.VMEM((2, ROWS, 8, PLANE), F32),
             pltpu.VMEM((2, ROWS, 8, PLANE), F32),
             dma,
+            dma,
             dma((CHUNKS,)),
-            dma((CHUNKS,)),
-            dma((CHUNKS,)),
-            dma((CHUNKS,)),
+            dma,
+            dma((CHUNKS // 2,)),
             dma((2,)),
             dma((2,)),
-            dma((2,)),
-            dma((2,)),
+            dma((6,)),
+            dma((6,)),
         ],
         compiler_params=pltpu.CompilerParams(
             collective_id=0, has_side_effects=True, vmem_limit_bytes=32 << 20

time: 24.4 us -> 23.8 us (0.975)
  the two profiles are of different devices: /device:TPU:70 before, /device:TPU:102 now
where the time goes in v5:
time: 23.8 us; the launch traced here: 23.7 us
  Pallas kernels  22.7 us (95%)
  local copies, waits for them, and re-layouts  0.97 us (4%)
    pallas_call x1, Pallas kernels, local(): pl.pallas_call(functools.partial(kernel, nv, nc), out_shape=jax.ShapeDtyp...  22.7 us
    unnamed x1, local copies, waits for them, and re-layouts  0.97 us

profile of v5, /device:TPU:102, one launch (start us, length us, event | category | flops | bytes accessed | tf_op | source)
XLA Modules:
  0.0 23.7 jit_solution(17433249503060318680)
XLA Ops:
  0.0 22.7 %shard_map.17 = f32[2,32,32,128]{3,2,1,0:T(8,128)S(1)} custom-call(bf16[2,32,32,128]{3,2,1,0:T(8,128)(2,1)} %f_hbm.1), custom_call_target="tpu_custom_call" | custom-call | flops 60000000 | bytes 1600000 | tf_op jit(solution)/shard_map/pallas_call | solution.py:596
  22.7 1.0 %copy.3 = f32[2,32,32,128]{3,2,1,0:T(8,128)} copy(f32[2,32,32,128]{3,2,1,0:T(8,128)S(1)} %shard_map.17) | data formatting | bytes 2097152

commit v6 on v5

--- a/solution.py
+++ b/solution.py
@@ -18,7 +18,7 @@
 H_STEPS = V // H_CHUNK
 BEFORE = 3
 FIRST = 6
-FLIGHT = 8
+SECOND = 11
 PLANE = V * Y
 
 
@@ -78,6 +78,7 @@
     pack_rs,
     cols_s,
     cols_r,
+    ready,
 ):
     vi = lax.axis_index("views")
     cj = lax.axis_index("cols")
@@ -99,8 +100,24 @@
     def greet(there):
         pl.semaphore_signal(barrier, inc=1, device_id=there, device_id_type=MESH)
 
+    middle = nc // 2
+    is_even = lax.rem(cj, 2) == 0
+    late_l = jnp.logical_and(has_left, jnp.logical_and(is_even, cj != middle))
+    late_r = jnp.logical_and(has_right, jnp.logical_or(is_even, cj == middle - 1))
+    early_l = jnp.logical_and(has_left, jnp.logical_not(late_l))
+    early_r = jnp.logical_and(has_right, jnp.logical_not(late_r))
+    late_z = jnp.logical_and(has_far, odd == 0)
+    early_z = jnp.logical_and(sends_far, odd == 0)
+    late_q = jnp.logical_and(sends_far, odd == 1)
+    early_q = jnp.logical_and(has_far, odd == 1)
+
     greet((partner, cj))
-    for exists, there in ((has_far, (behind, cj)), (has_left, (vi, left)), (has_right, (vi, right))):
+    for exists, there in (
+        (early_z, (ahead, cj)),
+        (early_q, (behind, cj)),
+        (early_l, (vi, left)),
+        (early_r, (vi, right)),
+    ):
 
         @pl.when(exists)
         def _():
@@ -157,21 +174,27 @@
     four = jnp.where(row8 < 4, pltpu.roll(packed[:8], 6, 0), pltpu.roll(packed[8:], 2, 0))
     own_cols[...] = folded(four)
 
-    one = jnp.int32(1)
-    pl.semaphore_wait(
-        barrier,
-        one
-        + jnp.where(sends_far, 1, 0)
-        + jnp.where(has_left, 1, 0)
-        + jnp.where(has_right, 1, 0),
-    )
-    @pl.when(has_left)
+    greeted = jnp.int32(1)
+    for late in (late_z, late_q, late_l, late_r):
+        greeted = greeted + jnp.where(late, 1, 0)
+    pl.semaphore_wait(barrier, greeted)
+
+    def tell(which, there):
+        pl.semaphore_signal(ready.at[which], inc=1, device_id=there, device_id_type=MESH)
+
+    @pl.when(late_l)
     def _():
         to_left.start()
-
-    @pl.when(has_right)
+        tell(1, (vi, left))
+
+    @pl.when(late_r)
     def _():
         to_right.start()
+        tell(0, (vi, right))
+
+    @pl.when(late_z)
+    def _():
+        tell(2, (behind, cj))
 
     cols_near = remote(own_cols, cols_in.at[1, odd], cols_s.at[0], cols_r.at[0], (partner, cj))
     cols_far = remote(cols_in.at[1, even], cols_in.at[1, odd], cols_s.at[1], cols_r.at[1], (ahead, cj))
@@ -264,6 +287,20 @@
     zeros = [jnp.zeros((Y, X), F32)] * 3
     lax.fori_loop(0, 2 * H_STEPS, horizontal, (zeros, zeros))
 
+    @pl.when(early_l)
+    def _():
+        pl.semaphore_wait(ready.at[0], 1)
+        to_left.start()
+
+    @pl.when(early_r)
+    def _():
+        pl.semaphore_wait(ready.at[1], 1)
+        to_right.start()
+
+    @pl.when(early_z)
+    def _():
+        pl.semaphore_wait(ready.at[2], 1)
+
     cols_near.wait_recv()
 
     @pl.when(sends_far)
@@ -280,15 +317,11 @@
 
     @pl.when(held)
     def _():
-        for k in range(FIRST, FLIGHT):
+        for k in range(FIRST, SECOND):
             near(k).start()
 
     def relay(k):
         near_in(k).wait_recv()
-
-        @pl.when(jnp.logical_and(held, k + FLIGHT < CHUNKS))
-        def _():
-            near(k + FLIGHT).start()
 
         @pl.when(sends_far)
         def _():
@@ -379,10 +412,27 @@
     def smooth_by(by, a):
         return by(a, -1) + (a + a) + by(a, 1)
 
-    relay(0)
-    relay(1)
-    relay(2)
-
+    for k in range(4):
+        relay(k)
+
+    @pl.when(has_far)
+    def _():
+        cols_far.wait_recv()
+
+        @pl.when(has_left)
+        def _():
+            far_left.start()
+
+        @pl.when(has_right)
+        def _():
+            far_right.start()
+
+    @pl.when(held)
+    def _():
+        for k in range(SECOND, CHUNKS):
+            near(k).start()
+
+    relay(4)
     @pl.when(has_left)
     def _():
         to_right.wait_recv()
@@ -421,24 +471,11 @@
             )
             edge_j[side, u] = w
             edge_d[side, u] = m
-        relay(3 + side)
+        relay(5 + side)
         return carry
 
     lax.fori_loop(0, 2, edges_h, 0)
 
-    @pl.when(has_far)
-    def _():
-        cols_far.wait_recv()
-
-        @pl.when(has_left)
-        def _():
-            far_left.start()
-
-        @pl.when(has_right)
-        def _():
-            far_right.start()
-
-    relay(5)
 
     def arrived(g):
         @pl.when(has_far)
@@ -449,7 +486,10 @@
             ).wait_recv()
 
     def start(g, carry):
-        relay(2 * g + 6)
+        @pl.when(g > 0)
+        def _():
+            relay(2 * g + 6)
+
         relay(2 * g + 7)
         arrived(g)
         vertical(g * STEP)
@@ -625,6 +665,7 @@
             dma((2,)),
             dma((6,)),
             dma((6,)),
+            pltpu.SemaphoreType.REGULAR((3,)),
         ],
         compiler_params=pltpu.CompilerParams(
             collective_id=0, has_side_effects=True, vmem_limit_bytes=32 << 20

time: 23.8 us -> 23.8 us (level)
  no operation moved by 1% of the time
where the time goes in v6:
time: 23.8 us; the launch traced here: 23.7 us
  Pallas kernels  22.7 us (95%)
  local copies, waits for them, and re-layouts  0.97 us (4%)
    pallas_call x1, Pallas kernels, local(): pl.pallas_call(functools.partial(kernel, nv, nc), out_shape=jax.ShapeDtyp...  22.7 us
    unnamed x1, local copies, waits for them, and re-layouts  0.97 us

profile of v6, /device:TPU:102, one launch (start us, length us, event | category | flops | bytes accessed | tf_op | source)
XLA Modules:
  0.0 23.7 jit_solution(16814074898581843410)
XLA Ops:
  0.0 22.7 %shard_map.17 = f32[2,32,32,128]{3,2,1,0:T(8,128)S(1)} custom-call(bf16[2,32,32,128]{3,2,1,0:T(8,128)(2,1)} %f_hbm.1), custom_call_target="tpu_custom_call" | custom-call | flops 60000000 | bytes 1600000 | tf_op jit(solution)/shard_map/pallas_call | solution.py:636
  22.7 1.0 %copy.3 = f32[2,32,32,128]{3,2,1,0:T(8,128)} copy(f32[2,32,32,128]{3,2,1,0:T(8,128)S(1)} %shard_map.17) | data formatting | bytes 2097152

commit v7 on v6

--- a/solution.py
+++ b/solution.py
@@ -536,6 +536,7 @@
             edge[side, 5] = edge[side, 3]
 
     def edges(side, carry):
+        relay(2 * BEFORE + 6 + side)
         j_below = jnp.where(jnp.logical_and(final, side == 1), 4, 8)
         q_from = jnp.where(jnp.logical_and(first, side == 0), 4, 0)
         tiles = [edge[side, r] for r in range(6)]
@@ -558,7 +559,6 @@
             depth = joined + 0.2 * (flux_x - cols_by(flux_x, -1) + flux_y - y_by(flux_y, -1))
             edge_j[side, u] = pltpu.roll(joined, 4, 0)
             edge_d[side, u] = pltpu.roll(depth, 5, 0)
-        relay(2 * BEFORE + 6 + side)
         return carry
 
     lax.fori_loop(0, 2, edges, 0)
@@ -582,14 +582,15 @@
             fix[u, pl.ds(4 * b, 4)] = block.T.reshape(4, Y, X)
         return carry
 
+    relay(2 * BEFORE + 8)
     lax.fori_loop(0, 2, spread_out, 0)
 
     def finish(g, carry):
         for k in range(2):
 
-            @pl.when(2 * g + k + 8 < CHUNKS)
+            @pl.when(2 * g + k + 9 < CHUNKS)
             def _():
-                relay(2 * g + k + 8)
+                relay(2 * g + k + 9)
 
         def varied(i, c):
             variation(i * STEP)

time: 23.8 us -> 23.5 us (0.987)
  Pallas kernels: 22.7 us -> 22.4 us
    pallas_call x1, Pallas kernels: 22.7 us -> 22.4 us  [local(): pl.pallas_call(functools.partial(kernel, nv, nc), out_shape=jax.ShapeDtyp...]
where the time goes in v7:
time: 23.5 us; the launch traced here: 23.3 us
  Pallas kernels  22.4 us (95%)
  local copies, waits for them, and re-layouts  0.97 us (4%)
    pallas_call x1, Pallas kernels, local(): pl.pallas_call(functools.partial(kernel, nv, nc), out_shape=jax.ShapeDtyp...  22.4 us
    unnamed x1, local copies, waits for them, and re-layouts  0.97 us

profile of v7, /device:TPU:102, one launch (start us, length us, event | category | flops | bytes accessed | tf_op | source)
XLA Modules:
  0.0 23.3 jit_solution(2264615679111719878)
XLA Ops:
  0.0 22.4 %shard_map.17 = f32[2,32,32,128]{3,2,1,0:T(8,128)S(1)} custom-call(bf16[2,32,32,128]{3,2,1,0:T(8,128)(2,1)} %f_hbm.1), custom_call_target="tpu_custom_call" | custom-call | flops 60000000 | bytes 1600000 | tf_op jit(solution)/shard_map/pallas_call | solution.py:637
  22.4 1.0 %copy.3 = f32[2,32,32,128]{3,2,1,0:T(8,128)} copy(f32[2,32,32,128]{3,2,1,0:T(8,128)S(1)} %shard_map.17) | data formatting | bytes 2097152

commit v8 on v7

--- a/solution.py
+++ b/solution.py
@@ -328,23 +328,23 @@
             far(k).start()
 
 
-    lane = lax.broadcasted_iota(jnp.int32, (STEP, 8, X), 2)
-    sub = lax.broadcasted_iota(jnp.int32, (STEP, 8, X), 1)
+    lane = lax.broadcasted_iota(jnp.int32, (STEP, Y, X), 2)
+    sub = lax.broadcasted_iota(jnp.int32, (STEP, Y, X), 1)
     rim = jnp.logical_or(lane < 2, lane >= X - 2)
     outer = jnp.logical_or(lane == 0, lane == X - 1)
 
     def parts(ref, *at):
-        return [ref[(*at, pl.ds(p, 8, stride=4), slice(None))] for p in range(4)]
+        return [ref[at]]
 
     def y_up(a, rest=0.0):
-        return a[1:] + [jnp.where(sub == 7, rest, pltpu.roll(a[0], 7, 1))]
+        return [jnp.where(sub == Y - 1, rest, pltpu.roll(a[0], Y - 1, 1))]
 
     def y_down(a):
-        return [jnp.where(sub == 0, 0.0, pltpu.roll(a[3], 1, 1))] + a[:3]
+        return [jnp.where(sub == 0, 0.0, pltpu.roll(a[0], 1, 1))]
 
     def smooth_y(a):
         pair = [b + c for b, c in zip(a, y_down(a))]
-        return [b + c for b, c in zip(pair, y_up(pair, a[3]))]
+        return [b + c for b, c in zip(pair, y_up(pair, a[0]))]
 
     def vertical(v0):
         span = pl.ds(v0, STEP)
@@ -376,14 +376,13 @@
             ]
             past = pl.ds(v0 + 1, STEP)
             w, m = parts(weight, u, past), parts(moment, u, past)
-            for p in range(4):
-                slope[u, span, p] = join(w[p], m[p], *(c[p] for c in tensor))
+            slope[u, span] = join(w[0], m[0], *(c[0] for c in tensor))
 
     def variation(v0):
         span = pl.ds(v0, STEP)
         for u in range(ROWS):
             t = parts(fix, u, span)
-            joined = [jnp.where(rim, t[p], slope[u, span, p]) for p in range(4)]
+            joined = [jnp.where(rim, t[0], slope[u, span])]
             flux_x, flux_y = [], []
             for here, below in zip(joined, y_up(joined)):
                 step_x = lanes(here, 1) - here
@@ -393,7 +392,7 @@
                 flux_y.append(step_y * scale)
             for p, above in enumerate(y_down(flux_y)):
                 depth = joined[p] + 0.2 * (flux_x[p] - lanes(flux_x[p], -1) + flux_y[p] - above)
-                out[u, span, pl.ds(p, 8, stride=4), :] = jnp.where(outer, lanes(t[p], -63), depth)
+                out[u, span] = jnp.where(outer, lanes(t[p], -63), depth)
 
     place = lax.broadcasted_iota(jnp.int32, (8, PLANE), 1)
     y_at = lax.rem(place, Y)
@@ -647,7 +646,7 @@
             pltpu.VMEM((ROWS, V + 1, Y, X), F32),
             pltpu.VMEM((ROWS, V + 1, Y, X), F32),
             pltpu.VMEM(block, F32),
-            pltpu.VMEM((ROWS, V, 4, 8, X), F32),
+            pltpu.VMEM(block, F32),
             pltpu.VMEM((16, PLANE), BF16),
             pltpu.VMEM((2, 16, PLANE // 2), BF16),
             pltpu.VMEM((16, PLANE // 2), BF16),

time: 23.5 us -> 23.7 us (level)
  no operation moved by 1% of the time
where the time goes in v8:
time: 23.7 us; the launch traced here: 23.5 us
  Pallas kernels  22.6 us (95%)
  local copies, waits for them, and re-layouts  0.97 us (4%)
    pallas_call x1, Pallas kernels, local(): pl.pallas_call(functools.partial(kernel, nv, nc), out_shape=jax.ShapeDtyp...  22.6 us
    unnamed x1, local copies, waits for them, and re-layouts  0.97 us

profile of v8, /device:TPU:102, one launch (start us, length us, event | category | flops | bytes accessed | tf_op | source)
XLA Modules:
  0.0 23.5 jit_solution(13123943171630610919)
XLA Ops:
  0.0 22.6 %shard_map.17 = f32[2,32,32,128]{3,2,1,0:T(8,128)S(1)} custom-call(bf16[2,32,32,128]{3,2,1,0:T(8,128)(2,1)} %f_hbm.1), custom_call_target="tpu_custom_call" | custom-call | flops 60000000 | bytes 1600000 | tf_op jit(solution)/shard_map/pallas_call | solution.py:636
  22.6 1.0 %copy.3 = f32[2,32,32,128]{3,2,1,0:T(8,128)} copy(f32[2,32,32,128]{3,2,1,0:T(8,128)S(1)} %shard_map.17) | data formatting | bytes 2097152

commit v9 on v8

--- a/solution.py
+++ b/solution.py
@@ -17,8 +17,8 @@
 H_CHUNK = 8
 H_STEPS = V // H_CHUNK
 BEFORE = 3
-FIRST = 6
-SECOND = 11
+FIRST = 5
+SECOND = 12
 PLANE = V * Y
 
 

time: 23.7 us -> 23.6 us (level)
  no operation moved by 1% of the time
where the time goes in v9:
time: 23.6 us; the launch traced here: 23.5 us
  Pallas kernels  22.5 us (95%)
  local copies, waits for them, and re-layouts  0.97 us (4%)
    pallas_call x1, Pallas kernels, local(): pl.pallas_call(functools.partial(kernel, nv, nc), out_shape=jax.ShapeDtyp...  22.5 us
    unnamed x1, local copies, waits for them, and re-layouts  0.97 us

profile of v9, /device:TPU:102, one launch (start us, length us, event | category | flops | bytes accessed | tf_op | source)
XLA Modules:
  0.0 23.5 jit_solution(1922538253192846562)
XLA Ops:
  0.0 22.5 %shard_map.17 = f32[2,32,32,128]{3,2,1,0:T(8,128)S(1)} custom-call(bf16[2,32,32,128]{3,2,1,0:T(8,128)(2,1)} %f_hbm.1), custom_call_target="tpu_custom_call" | custom-call | flops 60000000 | bytes 1600000 | tf_op jit(solution)/shard_map/pallas_call | solution.py:636
  22.5 1.0 %copy.3 = f32[2,32,32,128]{3,2,1,0:T(8,128)} copy(f32[2,32,32,128]{3,2,1,0:T(8,128)S(1)} %shard_map.17) | data formatting | bytes 2097152
